TPU v7x, 128 devices: a whole 4x4x4 slice. The times are simulated.
128 devices in a mesh: tomo: 8 (over y_hi, x), orient: 16 (over z, y_lo, core).
Axes of the slice: x: 4, y: 4 (y_hi: 2, y_lo: 2; y = y_hi * 2 + y_lo), z: 4, core: 2. Of those that a mesh axis runs over, the one named last changes fastest.
Arguments:
- subtomograms: bfloat16 [768, 64, 4096], P(('tomo', 'orient')), may hold values from -6 to 6
- rotated_refs: bfloat16 [64, 64, 4096], P('orient'), may hold values from -6 to 6
- wedges: bfloat16 [16, 64, 4096], P('tomo'), may hold values from 0 to 1, as said below
- ref_pick: int32 [2], replicated, may hold values from 0 to 63
- best_pick: int32 [768], P(('tomo', 'orient')), may hold values from 0 to 23
- class_of: int32 [768, 1], P(('tomo', 'orient')), may hold values from 0 to 15; in each aligned block of 6 rows (0 to 5, 6 to 11, ...) at most 3 rows name the same one
Outputs:
- scores: float32 [2, 768], P(None, ('tomo', 'orient'))
- averages: float32 [16, 64, 4096], P('orient', 'tomo')
Inputs may be any that keep to these rules, and one draw needn't show every extreme that they name: `class_of`: of the 6 subtomograms of one device at most 3 share a class, and some device has 3 in one class; every class has a subtomogram. `wedges`: each tomogram's weights are zero on a missing wedge of frequencies.
All inputs are finite; a program needn't handle non-finite values.
Results may differ from a plain program's by a relative error of at most 0.015.
Values may be sent and summed in bfloat16 or wider, within the bound.
A program may use at most 256 MiB of HBM per device.

v0:
```python
import functools

import jax
import jax.numpy as jnp
import numpy as np
from jax import lax
from jax.experimental import pallas as pl
from jax.experimental.pallas import tpu as pltpu
from jax.sharding import PartitionSpec as P

STEPS = 2
CLASSES = 16
N = 64
BF = jnp.bfloat16
F32 = jnp.float32


def score_tables():
    i = np.arange(N)
    ang = (i[:, None] * i[None, :] % N) * (2.0 * np.pi / N)
    c, s = np.cos(ang), np.sin(ang)
    c[np.abs(c) < 1e-9] = 0.0
    s[np.abs(s) < 1e-9] = 0.0
    h = N // 2
    eye, rev = np.eye(N), np.eye(N)[(-i) % N]

    def pairs(m00, m01, m10, m11):
        return np.array([[m00, m01], [m10, m11]])

    def lanes_forward(b):
        t = np.einsum("abzk,qr,hg->qahzbgrk", b, np.eye(2), np.eye(2))
        return t.reshape(512, 512)

    def rows_forward(b):
        t = np.transpose(b, (1, 3, 0, 2)).reshape(2, N, 2, h, 2)
        return np.transpose(t, (0, 1, 2, 4, 3)).reshape(128, 128)

    fwd = pairs(c, -s, s, c)
    wdg = pairs(eye, 0 * eye, 0 * eye, rev)
    inv = pairs(c, s, -s, c)
    x_fwd = np.concatenate([c[:h], -s[:h]], 0)
    x_fwd[h] = c[h]
    x_wdg = np.concatenate([eye[:h], rev[:h]], 0)
    x_wdg[h] = eye[h]
    y_inv = np.transpose(inv, (1, 3, 0, 2)).reshape(128, 128)
    z_inv = np.einsum("abzk,qr->aqzbrk", inv, np.eye(2)).reshape(256, 256)
    x_inv = x_fwd.T
    flip_rows = np.kron(np.diag([1.0, -1.0]), rev)
    flip_lanes = np.kron(np.eye(2), rev)
    return [
        np.stack([x_fwd, x_wdg]),
        np.stack([lanes_forward(fwd), lanes_forward(wdg)]),
        np.stack([rows_forward(fwd), rows_forward(wdg)]),
        y_inv, z_inv, x_inv, flip_rows, flip_lanes,
    ]


def dot(a, b):
    return jnp.dot(a, b, preferred_element_type=F32)


def forward(first, second, tx, tz, ty, left, plane, out):
    for q, vol in enumerate((first, second)):
        def x_pass(c, _):
            at = pl.multiple_of(c * 512, 512)
            r = dot(tx, vol[:, pl.ds(at, 512)]).astype(BF)
            for k in range(4):
                rows = pl.ds(pl.multiple_of((c * 4 + k) * 32, 32), 32)
                left[rows, q * 256:q * 256 + 128] = r[:32, k * 128:k * 128 + 128]
                left[rows, q * 256 + 128:q * 256 + 256] = r[32:, k * 128:k * 128 + 128]
            return 0
        lax.fori_loop(0, 8, x_pass, 0, unroll=8)

    def z_pass(m, _):
        at = pl.multiple_of(m * 128, 128)
        r = dot(left[pl.ds(at, 128), :], tz)
        for col in range(4):
            plane[pl.ds(col * 1024 + at, 128), :] = r[:, col * 128:col * 128 + 128]
        return 0
    lax.fori_loop(0, 8, z_pass, 0, unroll=8)

    def y_pass(m, _):
        d = jnp.concatenate(
            [plane[pl.ds(2 * m + k, 128, stride=32), :] for k in range(2)], 1).astype(BF)
        r = dot(ty, d).astype(BF)
        for k in range(2):
            out[pl.ds(pl.multiple_of((2 * m + k) * 128, 128), 128), :] = r[:, k * 128:k * 128 + 128]
        return 0
    lax.fori_loop(0, 16, y_pass, 0, unroll=16)


def mirror(g, flip_rows, flip_lanes):
    return dot(dot(flip_rows, g).astype(BF), flip_lanes)


def split(g, t):
    gr, gi, tr, ti = g[:64], g[64:], t[:64], t[64:]
    return (0.5 * (gr + tr), 0.5 * (gi + ti)), (0.5 * (gi - ti), -0.5 * (gr - tr))


def fold(v):
    return functools.reduce(jnp.add, [v[8 * k:8 * k + 8] for k in range(v.shape[0] // 8)])


def power(spec, twin, weight, edge):
    a, b = split(spec[0:128, :].astype(F32), twin)
    total = fold(edge[0:64, :] * (a[0] ** 2 + a[1] ** 2) + edge[64:128, :] * (b[0] ** 2 + b[1] ** 2))

    def body(kx, total):
        v = spec[pl.ds(pl.multiple_of(kx * 128, 128), 128), :].astype(F32)
        w = weight[pl.ds(pl.multiple_of(kx * 64, 64), 64), :]
        return total + fold(w * (v[:64] ** 2 + v[64:] ** 2))
    return lax.fori_loop(1, 32, body, total, unroll=31)


def wedge_setup(spec, flip_rows, flip_lanes, weight, edge):
    g = spec[0:128, :]
    t = mirror(g, jnp.abs(flip_rows), flip_lanes)
    edge[...] = 0.5 * (g.astype(F32) + t)

    def body(kx, _):
        v = spec[pl.ds(pl.multiple_of(kx * 128, 128), 128), :].astype(F32)
        weight[pl.ds(pl.multiple_of(kx * 64, 64), 64), :] = v[:64] + v[64:]
        return 0
    lax.fori_loop(1, 32, body, 0)


def spread_half(v, s, low):
    r = pltpu.roll(v, 64, 1)
    return jnp.where(low, v, r) if s == 0 else jnp.where(low, r, v)


def reference_setup(spec, twin, weight, edge, low, filt, extra):
    a, b = split(spec[0:128, :].astype(F32), twin)
    w0, w32 = edge[0:64, :], edge[64:128, :]
    for s in range(2):
        p = [spread_half(v, s, low) for v in (w0 * a[0], -w0 * a[1])]
        q = [spread_half(v, s, low) for v in (w32 * b[0], -w32 * b[1])]
        for k in range(2):
            filt[s, 64 * k:64 * k + 64, :] = 0.5 * (p[k] + q[k])
            extra[s, 64 * k:64 * k + 64, :] = 0.5 * (p[k] - q[k])

    def body(kx, _):
        v = spec[pl.ds(pl.multiple_of(kx * 128, 128), 128), :].astype(F32)
        w = weight[pl.ds(pl.multiple_of(kx * 64, 64), 64), :]
        re, im = w * v[:64], -w * v[64:]
        for s in range(2):
            filt[s, pl.ds(pl.multiple_of(kx * 128, 128), 64), :] = spread_half(re, s, low)
            filt[s, pl.ds(pl.multiple_of(kx * 128 + 64, 64), 64), :] = spread_half(im, s, low)
        return 0
    lax.fori_loop(1, 32, body, 0)


def correlate(spec, twin, filt, extra, ty, tz, tx, left, plane):
    def times(v, w):
        return (v[:64] * w[:64] - v[64:] * w[64:], v[:64] * w[64:] + v[64:] * w[:64])

    def cross(kx):
        at = pl.multiple_of(kx * 128, 128)
        return times(spec[pl.ds(at, 128), :].astype(F32), filt[pl.ds(at, 128), :])

    def finish(m, parts):
        d = jnp.concatenate([jnp.concatenate(p, 0).astype(BF) for p in parts], 1)
        r = dot(ty, d).astype(BF)
        for k in range(2):
            rows = pl.ds(pl.multiple_of((2 * m + k) * 64, 64), 64)
            left[rows, 0:128] = r[:64, k * 128:k * 128 + 128]
            left[rows, 128:256] = r[64:, k * 128:k * 128 + 128]

    c0, e0 = cross(0), times(twin, extra)
    finish(0, [(c0[0] + e0[0], c0[1] + e0[1]), cross(1)])

    def y_pass(m, _):
        finish(m, [cross(2 * m), cross(2 * m + 1)])
        return 0
    lax.fori_loop(1, 16, y_pass, 0, unroll=15)

    def z_pass(m, _):
        at = pl.multiple_of(m * 256, 256)
        r = dot(left[pl.ds(at, 256), 0:256], tz)
        for p in range(2):
            plane[pl.ds(p * 2048 + at, 256), :] = r[:, p * 128:p * 128 + 128]
        return 0
    lax.fori_loop(0, 8, z_pass, 0, unroll=8)

    def x_pass(m, top):
        d = jnp.concatenate(
            [plane[pl.ds(2 * m + k, 64, stride=64), :] for k in range(2)], 1).astype(BF)
        r = dot(tx, d)
        return jnp.maximum(top, jnp.maximum(r[:, :128], r[:, 128:]))
    top = lax.fori_loop(0, 32, x_pass, jnp.full((64, 128), -jnp.inf, F32), unroll=16)
    return functools.reduce(jnp.maximum, [top[8 * k:8 * k + 8] for k in range(8)])


def score_kernel(v, refs, wedge, txf, tzf, tyf, tyi, tzi, txi, fr, fl, out,
                 left, plane, spec, rspec, twin, weight, edge, filt, extra):
    low = lax.broadcasted_iota(jnp.int32, (64, 128), 1) < 64
    low8 = low[:8]

    def halves(t, op, fill):
        f = jnp.max if op == "max" else jnp.sum
        return [f(jnp.where(low8 == (k == 0), t, fill), keepdims=True) for k in range(2)]

    forward(wedge, wedge, txf[1], tzf[1], tyf[1], left, plane, rspec)
    wedge_setup(rspec, fr[...], fl[...], weight, edge)
    forward(refs.at[0], refs.at[1], txf[0], tzf[0], tyf[0], left, plane, rspec)
    rt = mirror(rspec[0:128, :], fr[...], fl[...])
    rp = halves(power(rspec, rt, weight, edge), "sum", 0.0)
    reference_setup(rspec, rt, weight, edge, low, filt, extra)
    row = lax.broadcasted_iota(jnp.int32, (8, 128), 0)
    lane = lax.broadcasted_iota(jnp.int32, (8, 128), 1)

    def one_pair(pair, result):
        forward(v.at[2 * pair], v.at[2 * pair + 1], txf[0], tzf[0], tyf[0], left, plane, spec)
        t = mirror(spec[0:128, :], fr[...], fl[...])
        own = halves(power(spec, t, weight, edge), "sum", 0.0)

        def one_step(s, result):
            top = halves(correlate(spec, t, filt.at[s], extra[s], tyi[...], tzi[...], txi[...], left, plane), "max", -jnp.inf)
            for k in range(2):
                norm = jnp.sqrt(own[k] * jnp.where(s == 0, rp[0], rp[1]) / float(N ** 3) + 1e-6)
                result = jnp.where((row == s) & (lane == 2 * pair + k), top[k] / norm, result)
            return result
        return lax.fori_loop(0, 2, one_step, result)
    out[...] = lax.fori_loop(0, 3, one_pair, jnp.zeros((8, 128), F32))


def scores_call(v, refs, wedge):
    tables = [jnp.asarray(t, dtype=BF) for t in score_tables()]
    return pl.pallas_call(
        score_kernel,
        out_shape=jax.ShapeDtypeStruct((8, 128), F32),
        in_specs=[pl.BlockSpec(memory_space=pltpu.VMEM)] * 11,
        out_specs=pl.BlockSpec(memory_space=pltpu.VMEM),
        scratch_shapes=[
            pltpu.VMEM((2048, 512), BF), pltpu.VMEM((4096, 128), F32),
            pltpu.VMEM((4096, 128), BF), pltpu.VMEM((4096, 128), BF),
            pltpu.VMEM((128, 128), F32), pltpu.VMEM((2048, 128), F32), pltpu.VMEM((128, 128), F32),
            pltpu.VMEM((2, 4096, 128), F32), pltpu.VMEM((2, 128, 128), F32),
        ],
        cost_estimate=pl.CostEstimate(flops=20 * 10**9, bytes_accessed=6 * 10**6, transcendentals=0),
        compiler_params=pltpu.CompilerParams(vmem_limit_bytes=50 * 2**20),
    )(v, refs, wedge, *tables)


def turn_tables():
    eye, rev = np.eye(N), np.eye(N)[::-1]
    two, swap = np.eye(2), np.eye(2)[::-1]
    pair = np.concatenate([eye, eye], 1)
    lanes = np.einsum("ac,hg,zw->ahzgcw", two, two, eye).reshape(256, 256)
    rows = np.transpose(eye.reshape(N, 32, 2), (0, 2, 1)).reshape(N, N)
    flip_rows = np.stack([eye, rev])
    flip_lanes = np.stack([np.kron(a, b) for a in (two, swap) for b in (eye, rev)])
    return [pair, lanes, rows, flip_rows, flip_lanes]


def turn_kernel(pick, classes, v, pair, lanes, rows, flip_rows, flip_lanes, out, held, wide, mixed, sums):
    low = lax.broadcasted_iota(jnp.int32, (64, 128), 1) < 64

    def clear(k, _):
        sums[pl.ds(pl.multiple_of(k * 512, 512), 512), :] = jnp.zeros((512, 128), F32)
        return 0
    lax.fori_loop(0, 64, clear, 0)

    def swap_ends():
        def body(m, _):
            blocks = []
            for k in range(2):
                blk = held[pl.ds(pl.multiple_of((2 * m + k) * 64, 64), 64), :].astype(F32)
                blocks += [jnp.where(low, blk, 0.0), jnp.where(low, 0.0, blk)]
            w = jnp.concatenate(blocks, 0).astype(BF)
            r = lax.dot_general(pair[...], w, (((1,), (1,)), ((), ())), preferred_element_type=F32).astype(BF)
            for k in range(2):
                held[pl.ds(pl.multiple_of((2 * m + k) * 64, 64), 64), :] = r[:, k * 128:k * 128 + 128]
            return 0
        lax.fori_loop(0, 16, body, 0, unroll=16)

    def swap_first():
        def widen(m, _):
            at = pl.ds(pl.multiple_of(m * 256, 256), 256)
            wide[at, :] = held[at, :].astype(F32)
            return 0
        lax.fori_loop(0, 8, widen, 0, unroll=8)

        def gather(m, _):
            d = [wide[pl.ds(2 * m + k, 32, stride=64), :] for k in range(2)]
            mixed[pl.ds(pl.multiple_of(m * 32, 32), 32), :] = jnp.concatenate(d, 1).astype(BF)
            return 0
        lax.fori_loop(0, 32, gather, 0, unroll=32)

        def body(m, _):
            r = dot(mixed[pl.ds(pl.multiple_of(m * 256, 256), 256), :], lanes[...]).astype(BF)
            halves = [jnp.concatenate([r[k * 32:k * 32 + 32, h * 128:h * 128 + 128] for k in range(8)], 1)
                      for h in range(2)]
            t = dot(rows[...], jnp.concatenate(halves, 0)).astype(BF)
            for k in range(8):
                held[pl.ds(pl.multiple_of((m * 8 + k) * 64, 64), 64), :] = t[:, k * 128:k * 128 + 128]
            return 0
        lax.fori_loop(0, 4, body, 0, unroll=4)

    def one(i, _):
        number = pick[i]
        order, place = number // 4, number % 4
        even = (order == 0) | (order == 3) | (order == 4)
        f0 = jnp.where(even, (place == 1) | (place == 2), (place == 0) | (place == 3)).astype(jnp.int32)
        f1 = place % 2
        f2 = place // 2
        for b in range(32):
            held[b * 64:b * 64 + 64, :] = v[i, :, b * 128:b * 128 + 128]
        pl.when((order == 1) | (order == 3) | (order == 5))(swap_ends)
        pl.when((order >= 1) & (order <= 4))(swap_first)
        pl.when((order == 1) | (order == 4))(swap_ends)
        c = classes[i]
        base = c * 2048
        j0, jl = flip_rows[f0], flip_lanes[f1 * 2 + f2]

        def flip_ends(m, _):
            at = pl.ds(pl.multiple_of(m * 256, 256), 256)
            held[at, :] = dot(held[at, :], jl).astype(BF)
            return 0

        @pl.when(f1 + f2 > 0)
        def _():
            lax.fori_loop(0, 8, flip_ends, 0, unroll=8)

        def add(m, flipped):
            blocks = []
            for k in range(4):
                b = m * 4 + k
                src = b + f1 * (31 - 2 * b)
                blocks.append(held[pl.ds(pl.multiple_of(src * 64, 64), 64), :])
            if flipped:
                u = dot(j0, jnp.concatenate(blocks, 1))
                blocks = [u[:, k * 128:k * 128 + 128] for k in range(4)]
            for k in range(4):
                at = pl.ds(base + m * 4 + k, 64, stride=32)
                sums[at, :] = sums[at, :] + blocks[k].astype(F32)

        @pl.when(f0 > 0)
        def _():
            lax.fori_loop(0, 8, lambda m, c: (add(m, True), c)[1], 0, unroll=8)

        @pl.when(f0 == 0)
        def _():
            lax.fori_loop(0, 8, lambda m, c: (add(m, False), c)[1], 0, unroll=8)
        return 0
    lax.fori_loop(0, 6, one, 0)

    def narrow(k, _):
        at = pl.ds(pl.multiple_of(k * 512, 512), 512)
        out[at, :] = sums[at, :].astype(BF)
        return 0
    lax.fori_loop(0, 64, narrow, 0)


def turn_call(v, pick, classes):
    tables = [jnp.asarray(t, dtype=BF) for t in turn_tables()]
    vm = pl.BlockSpec(memory_space=pltpu.VMEM)
    return pl.pallas_call(
        turn_kernel,
        out_shape=jax.ShapeDtypeStruct((32768, 128), BF),
        in_specs=[pl.BlockSpec(memory_space=pltpu.SMEM)] * 2 + [vm] * 6,
        out_specs=vm,
        scratch_shapes=[pltpu.VMEM((2048, 128), BF), pltpu.VMEM((2048, 128), F32), pltpu.VMEM((1024, 256), BF), pltpu.VMEM((32768, 128), F32)],
        compiler_params=pltpu.CompilerParams(vmem_limit_bytes=50 * 2**20),
    )(pick, classes, v, *tables)


def local(subtomograms, rotated_refs, wedges, ref_pick, best_pick, class_of):
    orient_size, orient_index = lax.axis_size("orient"), lax.axis_index("orient")
    per = rotated_refs.shape[0]
    wedge = lax.dynamic_index_in_dim(wedges, orient_index * wedges.shape[0] // orient_size, 0, False)
    mine = [
        jnp.where(
            ref_pick[s] // per == orient_index,
            lax.dynamic_index_in_dim(rotated_refs, ref_pick[s] % per, 0, False), 0
        ) for s in range(STEPS)
    ]
    refs = lax.psum(jnp.stack(mine), "orient")
    class_index = class_of[:, 0]
    sums = turn_call(subtomograms, best_pick, class_index)
    received = lax.all_to_all(sums.reshape(CLASSES, 2048, 128), "orient", split_axis=0, concat_axis=0, tiled=True)
    hits = class_index[None, :] == jnp.arange(CLASSES, dtype=jnp.int32)[:, None]
    counts = lax.psum(jnp.sum(hits.astype(F32), axis=1), ("tomo", "orient"))
    result = scores_call(subtomograms, refs, wedge)
    total = jnp.sum(received.astype(F32), axis=0).astype(BF)
    slab = lax.psum_scatter(total, "tomo", scatter_dimension=0, tiled=True).astype(F32)
    averages = (slab / lax.dynamic_index_in_dim(counts, orient_index, 0, False)).reshape(1, 8, 4096)
    return (result[:STEPS, :subtomograms.shape[0]], averages)


def solution(mesh):
    placed = (
        P(("tomo", "orient"), None, None),
        P("orient", None, None),
        P("tomo", None, None),
        P(),
        P(("tomo", "orient")),
        P(("tomo", "orient"), None),
    )
    return jax.shard_map(
        local,
        mesh=mesh,
        in_specs=placed,
        out_specs=(P(None, ("tomo", "orient")), P("orient", "tomo", None)),
        check_vma=False,
    )
```

profile of v0, /device:TPU:0, one launch (start us, length us, event | category | flops | bytes accessed | tf_op | source)
XLA Modules:
  0.0 299.5 jit_solution(5117505932627785153)
XLA Ops:
  8.0 0.0 copy-start
  8.0 0.0 copy-start.1
  8.0 2.0 copy-done.1
  10.0 0.9 copy-done.2
  10.9 0.9 copy-done.3
  11.8 0.8 copy-done.4
  12.6 0.7 copy-done.5
  13.3 0.7 copy-done.6
  14.0 0.7 copy-done.7
  14.7 0.7 copy-done.8
  15.3 23.6 %shard_map.195 = bf16[32768,128]{1,0:T(8,128)(2,1)} custom-call(s32[6]{0:T(128)S(1)} %copy-done.7, s32[6]{0:T(128)S(1)} %bitcast.7, bf16[6,64,4096]{2,1,0:T(8,128)(2,1)S(1)} %copy-done.1, bf16[64,128]{1,0:T(8,128)(2,1)S(1)} %copy-done.6, bf16[256,256]{1,0:T(8,128)(2,1)S(1)} %copy-done.3, bf16[64,64]{1,0:T(8,128)(2,1)S(1)} %copy-done.5, ...), custom_call_target="tpu_custom_call" | custom-call | tf_op jit(solution)/shard_map/pallas_call | solution.py:359
  38.9 7.0 %all-to-all-start = ((bf16[16,2048,128]{2,1,0:T(8,128)(2,1)}), bf16[16,2048,128]{2,1,0:T(8,128)(2,1)}, u32[]{:S(2)}, u32[]{:S(2)}) async-start(bf16[16,2048,128]{2,1,0:T(8,128)(2,1)} %bitcast.9), calls=%async_computation | async-start | bytes 16777216 | tf_op jit(solution)/shard_map/all_to_all | solution.py:382
  45.8 0.0 copy-start.9
  45.9 0.0 all-reduce.2.cloned.1.call-start
  45.9 0.0 copy-done.20
  45.9 0.6 fusion
  51.7 0.0 copy-done.19
  51.7 0.1 dynamic-slice_select_fusion.1
  51.8 1.1 pad_maximum_fusion
  52.9 0.0 all-reduce.2.cloned.1.call-update
  52.9 0.0 reduce-scatter.2.cloned.1.call-start
  53.0 0.0 copy-done.9
  53.0 0.1 convert_reduce_fusion
  53.1 161.2 %psum.15 = f32[16]{0:T(128)S(1)} all-reduce(f32[16]{0:T(128)S(1)} %convert_reduce_fusion), channel_id=1, replica_groups=mesh['tomo'=8,'orient'=16] {'tomo','orient'}, use_global_device_ids=true, to_apply=%region_4.5 | all-reduce | flops 16 | bytes 128 | tf_op jit(solution)/shard_map/psum | solution.py:384
  214.3 0.6 dynamic_slice.18
  214.9 0.0 copy-done
  215.0 0.0 copy-start.11
  215.0 0.0 copy-start.12
  215.0 0.0 copy-start.13
  215.0 0.0 copy-start.14
  215.0 0.0 copy-start.15
  215.0 0.0 copy-start.16
  215.0 0.0 copy-start.17
  215.1 0.0 copy-start.18
  215.1 0.0 all-to-all-done
  215.1 5.6 %reduce_sum.21 = bf16[2048,128]{1,0:T(8,128)(2,1)} reduce(bf16[16,2048,128]{2,1,0:T(8,128)(2,1)} %all-to-all-done, bf16[]{:T(256)} %constant.95.clone.1), dimensions={0}, to_apply=%region_1.2 | reduce | flops 3932160 | bytes 8912898 | tf_op jit(solution)/shard_map/reduce_sum | solution.py:386
  220.7 0.0 reduce-scatter.2.cloned.1.call-update
  220.7 0.0 all-reduce.2.cloned.1.call-done.refs
  220.7 0.0 copy-done.11
  220.8 0.0 copy-done.12
  220.8 0.0 copy-done.13
  220.8 0.0 copy-done.14
  220.8 1.2 copy-done.10
  222.1 33.7 %shard_map.194 = f32[8,128]{1,0:T(8,128)S(1)} custom-call(bf16[6,64,4096]{2,1,0:T(8,128)(2,1)} %v.3, bf16[2,64,4096]{2,1,0:T(8,128)(2,1)S(1)} %copy-done.10, bf16[64,4096]{1,0:T(8,128)(2,1)S(1)} %dynamic-slice_bitcast_fusion.wedge, bf16[2,64,64]{2,1,0:T(8,128)(2,1)S(1)} %copy-done.17, bf16[2,512,512]{2,1,0:T(8,128)(2,1)S(1)} %copy-done.11, ...), custom_call_target="tpu_custom_call" | custom-call | flops 20000000000 | bytes 6000000 | tf_op jit(solution)/shard_map/pallas_call | solution.py:230
  255.7 0.6 slice.13
  256.3 33.5 %reduce-scatter.2.cloned.1.call-done = bf16[256,128]{1,0:T(8,128)(2,1)} async-done(((bf16[2048,128]{1,0:T(8,128)(2,1)}), bf16[256,128]{1,0:T(8,128)(2,1)}) %reduce-scatter.2.cloned.1.call-update) | async-done | bytes 65552 | tf_op jit(solution)/shard_map/reduce_scatter | solution.py:387
  289.8 1.5 convert_divide_fusion
  291.3 0.7 reshape.12
  (15 shorter events, 0.1 us)
Async XLA Ops:
  8.0 206.9 %copy-start = (bf16[2,64,4096]{2,1,0:T(8,128)(2,1)S(1)}, bf16[2,64,4096]{2,1,0:T(8,128)(2,1)}, u32[]{:S(2)}) copy-start(bf16[2,64,4096]{2,1,0:T(8,128)(2,1)} %param.21) | copy-start | bytes 3145732
  8.0 2.0 copy-start.1
  10.0 0.9 copy-start.2
  10.9 0.9 copy-start.3
  11.8 0.8 copy-start.4
  12.6 0.7 copy-start.5
  13.3 0.7 copy-start.6
  14.0 0.7 copy-start.7
  14.7 0.7 copy-start.8
  38.9 7.0 %copy-start.20 = (s32[2]{0:T(128)S(1)}, s32[2]{0:T(128)}, u32[]{:S(2)}) copy-start(s32[2]{0:T(128)} %param.22) | copy-start | bytes 28
  38.9 12.9 %copy-start.19 = (bf16[4,64,4096]{2,1,0:T(8,128)(2,1)S(1)}, bf16[4,64,4096]{2,1,0:T(8,128)(2,1)}, u32[]{:S(2)}) copy-start(bf16[4,64,4096]{2,1,0:T(8,128)(2,1)} %param.20) | copy-start | bytes 6291460
  38.9 176.2 %all-to-all-start = ((bf16[16,2048,128]{2,1,0:T(8,128)(2,1)}), bf16[16,2048,128]{2,1,0:T(8,128)(2,1)}, u32[]{:S(2)}, u32[]{:S(2)}) async-start(bf16[16,2048,128]{2,1,0:T(8,128)(2,1)} %bitcast.9), calls=%async_computation | async-start | bytes 16777216 | tf_op jit(solution)/shard_map/all_to_all | solution.py:382
  45.8 7.2 %copy-start.9 = (s32[6,1]{0,1:T(1,128)S(1)}, s32[6,1]{0,1:T(1,128)}, u32[]{:S(2)}) copy-start(s32[6,1]{0,1:T(1,128)} %param.24) | copy-start | bytes 76
  45.9 174.9 %all-reduce.2.cloned.1.call-start = ((), (), s32[]{:S(2)}) async-start(), calls=%async_computation.2 | async-start | bytes 2097152 | tf_op jit(solution)/shard_map/psum | solution.py:379
  52.9 236.9 %reduce-scatter.2.cloned.1.call-start = ((), (), s32[]{:S(2)}) async-start(), calls=%async_computation.3 | async-start | bytes 589824 | tf_op jit(solution)/shard_map/reduce_scatter | solution.py:387
  215.0 5.8 %copy-start.11 = (bf16[2,512,512]{2,1,0:T(8,128)(2,1)S(1)}, bf16[2,512,512]{2,1,0:T(8,128)(2,1)}, u32[]{:S(2)}) copy-start(bf16[2,512,512]{2,1,0:T(8,128)(2,1)} %constant.105.clone.tzf) | copy-start | bytes 3145732
  215.0 5.8 %copy-start.12 = (bf16[256,256]{1,0:T(8,128)(2,1)S(1)}, bf16[256,256]{1,0:T(8,128)(2,1)}, u32[]{:S(2)}) copy-start(bf16[256,256]{1,0:T(8,128)(2,1)} %constant.108.clone.tzi) | copy-start | bytes 393220
  215.0 5.8 %copy-start.13 = (bf16[2,128,128]{2,1,0:T(8,128)(2,1)S(1)}, bf16[2,128,128]{2,1,0:T(8,128)(2,1)}, u32[]{:S(2)}) copy-start(bf16[2,128,128]{2,1,0:T(8,128)(2,1)} %constant.106.clone.tyf) | copy-start | bytes 196612
  215.0 5.8 %copy-start.14 = (bf16[128,128]{1,0:T(8,128)(2,1)S(1)}, bf16[128,128]{1,0:T(8,128)(2,1)}, u32[]{:S(2)}) copy-start(bf16[128,128]{1,0:T(8,128)(2,1)} %constant.111.clone.fl) | copy-start | bytes 98308
  215.0 5.8 %copy-start.15 = (bf16[128,128]{1,0:T(8,128)(2,1)S(1)}, bf16[128,128]{1,0:T(8,128)(2,1)}, u32[]{:S(2)}) copy-start(bf16[128,128]{1,0:T(8,128)(2,1)} %constant.110.clone.fr) | copy-start | bytes 98308
  215.0 5.8 %copy-start.16 = (bf16[128,128]{1,0:T(8,128)(2,1)S(1)}, bf16[128,128]{1,0:T(8,128)(2,1)}, u32[]{:S(2)}) copy-start(bf16[128,128]{1,0:T(8,128)(2,1)} %constant.107.clone.tyi) | copy-start | bytes 98308
  215.0 5.8 %copy-start.17 = (bf16[2,64,64]{2,1,0:T(8,128)(2,1)S(1)}, bf16[2,64,64]{2,1,0:T(8,128)(2,1)}, u32[]{:S(2)}) copy-start(bf16[2,64,64]{2,1,0:T(8,128)(2,1)} %constant.104.clone.txf) | copy-start | bytes 49156
  215.1 5.8 %copy-start.18 = (bf16[64,64]{1,0:T(8,128)(2,1)S(1)}, bf16[64,64]{1,0:T(8,128)(2,1)}, u32[]{:S(2)}) copy-start(bf16[64,64]{1,0:T(8,128)(2,1)} %constant.109.clone.txi) | copy-start | bytes 24580
  220.8 1.2 copy-start.10
Sparse Core Ops, SparseCore 0:
  53.1 131.3 all-reduce.1
Sparse Core Ops, SparseCore 1:
  220.8 69.0 reduce-scatter.1
where the time goes:
time: 300 us; the launch traced here: 299 us
  blocking collectives  161 us (54%)
  Pallas kernels  57.2 us (19%)
  waiting for transfers between devices  33.6 us (11%)
  between operations  21 us (7%)
  local copies, waits for them, and re-layouts  11 us (4%)
  other arithmetic  8.36 us (3%)
  starting transfers between devices  7.04 us (2%)
    psum x1, blocking collectives, local(): counts = lax.psum(jnp.sum(hits.astype(F32), axis=1), ('tomo', 'orient'))  161 us
    pallas_call x1, Pallas kernels, scores_call(): pl.pallas_call(score_kernel, out_shape=jax.ShapeDtypeStruct((8, 128), F32...  33.7 us
    reduce_scatter x1, waiting for transfers between devices, local(): lax.psum_scatter(total, 'tomo', scatter_dimension=0, tiled=True).astype(F32)  33.5 us
    pallas_call x1, Pallas kernels, turn_call(): pl.pallas_call(turn_kernel, out_shape=jax.ShapeDtypeStruct((32768, 128),...  23.6 us
    unnamed x42, local copies, waits for them, and re-layouts  8.58 us
    all_to_all x1, starting transfers between devices, local(): lax.all_to_all(sums.reshape(CLASSES, 2048, 128), 'orient', split_axis=0,...  6.96 us
  transfers between devices with their start and end apart: 3, of which 1 were waited for; matrix products, arithmetic and copies ran while one was open for 3% of the time, Pallas kernels for 11%

commit v1 on v0

--- a/solution.py
+++ b/solution.py
@@ -13,6 +13,7 @@
 N = 64
 BF = jnp.bfloat16
 F32 = jnp.float32
+MESH = pl.DeviceIdType.MESH
 
 
 def score_tables():
@@ -238,7 +239,6 @@
             pltpu.VMEM((128, 128), F32), pltpu.VMEM((2048, 128), F32), pltpu.VMEM((128, 128), F32),
             pltpu.VMEM((2, 4096, 128), F32), pltpu.VMEM((2, 128, 128), F32),
         ],
-        cost_estimate=pl.CostEstimate(flops=20 * 10**9, bytes_accessed=6 * 10**6, transcendentals=0),
         compiler_params=pltpu.CompilerParams(vmem_limit_bytes=50 * 2**20),
     )(v, refs, wedge, *tables)
 
@@ -311,7 +311,7 @@
         pl.when((order >= 1) & (order <= 4))(swap_first)
         pl.when((order == 1) | (order == 4))(swap_ends)
         c = classes[i]
-        base = c * 2048
+        base = ((c % 2) * 8 + c // 2) * 2048
         j0, jl = flip_rows[f0], flip_lanes[f1 * 2 + f2]
 
         def flip_ends(m, _):
@@ -366,6 +366,333 @@
     )(pick, classes, v, *tables)
 
 
+PARTS = (
+    ((0, 1, 2), False, 0, 48), ((0, 1, 2), True, 48, 32),
+    ((1, 2, 0), False, 80, 48), ((1, 2, 0), True, 128, 32),
+    ((2, 0, 1), False, 160, 48), ((2, 0, 1), True, 208, 48),
+)
+MOVES = 10
+
+
+class Place:
+    def __init__(self):
+        tomo, orient = lax.axis_index("tomo"), lax.axis_index("orient")
+        self.core = orient % 2
+        self.at = (orient // 4, (tomo // 4) * 2 + (orient // 2) % 2, tomo % 4)
+        self.near = tuple(c + 1 - 2 * (c % 2) for c in self.at)
+        self.far = tuple(3 - c for c in self.at)
+        self.cross = tuple((c + 2) % 4 for c in self.at)
+
+    def device(self, axis=None, to=None, core=None):
+        z, y, x = [to if axis == k else c for k, c in enumerate(self.at)]
+        core = self.core if core is None else core
+        return ((y // 2) * 4 + x, z * 4 + (y % 2) * 2 + core)
+
+    def other_core(self):
+        return self.device(core=1 - self.core)
+
+    def partners(self):
+        return [self.other_core()] + [self.device(k, t[k]) for k in range(3) for t in (self.near, self.far)]
+
+
+def greet(place):
+    barrier = pltpu.get_barrier_semaphore()
+    for device in place.partners():
+        pl.semaphore_signal(barrier, inc=1, device_id=device, device_id_type=MESH)
+    pl.semaphore_wait(barrier, 7)
+
+
+class ClassSums:
+    def __init__(self, place, sums, mine, got, keep, send, first, second, total, send_sem, recv_sem, load_sem):
+        self.p, self.sums, self.mine, self.got, self.keep, self.send = place, sums, mine, got, keep, send
+        self.first, self.second, self.total = first, second, total
+        self.send_sem, self.recv_sem = send_sem, recv_sem
+        self.load = pltpu.make_async_copy(sums.at[place.core], mine, load_sem)
+        self.sent = []
+        self.coming = {}
+
+    def move(self, part, k, src, dst, device):
+        copy = pltpu.make_async_remote_copy(
+            src_ref=src, dst_ref=dst, send_sem=self.send_sem.at[part * MOVES + k],
+            recv_sem=self.recv_sem.at[part * MOVES + k], device_id=device, device_id_type=MESH)
+        copy.start()
+        self.sent.append(copy)
+        self.coming[part, k] = copy
+
+    def start(self):
+        for i, (_, _, row, rows) in enumerate(PARTS):
+            cells = pl.ds(row, rows)
+            self.move(i, 0, self.sums.at[1 - self.p.core, :, cells, :], self.got.at[:, cells, :], self.p.other_core())
+        self.load.start()
+
+    def links(self, part, level):
+        axis = PARTS[part][0][level]
+        near, far = self.p.near[axis], self.p.far[axis]
+        f, g = (far, near) if PARTS[part][1] else (near, far)
+        return axis, self.p.at[axis], f, g, self.p.cross[axis]
+
+    def prefix(self, part, level):
+        base = 0
+        for k in range(level):
+            base = base + self.p.at[PARTS[part][0][k]] * 4 ** (2 - k)
+        return base, 4 ** (2 - level)
+
+    def halves(self, part, level, value):
+        _, _, row, rows = PARTS[part]
+        cells = pl.ds(row, rows)
+        axis, c, f, g, h = self.links(part, level)
+        base, size = self.prefix(part, level)
+        for slot, d in ((1, h), (0, f)):
+            def out(k, _, d=d):
+                at = base + d * size + k
+                self.send[at, cells, :] = value(d * size + k).astype(BF)
+                return 0
+            lax.fori_loop(0, size, out, 0, unroll=min(size, 4))
+            self.move(part, 1 + 3 * level + slot, self.send.at[pl.ds(base + d * size, size), cells, :],
+                      self.first[level].at[slot, :, cells, :], self.p.device(axis, f))
+        for d in (g, c):
+            def stay(k, _, d=d):
+                self.keep[base + d * size + k, cells, :] = value(d * size + k)
+                return 0
+            lax.fori_loop(0, size, stay, 0, unroll=min(size, 4))
+
+    def round(self, r):
+        for part in range(len(PARTS)):
+            self.step(r, part)
+
+    def step(self, r, part):
+        order, _, row, rows = PARTS[part]
+        cells = pl.ds(row, rows)
+        if r == 0:
+            if part == 0:
+                self.load.wait()
+            self.coming[part, 0].wait_recv()
+
+            def value(at):
+                d = (at // 16, at // 4 % 4, at % 4)
+                z, y, x = [d[order.index(k)] for k in range(3)]
+                src = (z * 2 + y % 2) * 8 + (y // 2) * 4 + x
+                return self.mine[src, cells, :].astype(F32) + self.got[src, cells, :].astype(F32)
+            self.halves(part, 0, value)
+            return
+        level = (r - 1) // 2
+        axis, c, f, g, h = self.links(part, level)
+        base, size = self.prefix(part, level)
+        if r % 2:
+            self.coming[part, 2 + 3 * level].wait_recv()
+
+            def body(k, _):
+                at = base + g * size + k
+                v = self.keep[at, cells, :] + self.first[level][1, k, cells, :].astype(F32)
+                self.send[at, cells, :] = v.astype(BF)
+                return 0
+            lax.fori_loop(0, size, body, 0, unroll=min(size, 4))
+            self.move(part, 3 + 3 * level, self.send.at[pl.ds(base + g * size, size), cells, :],
+                      self.second[level].at[:, cells, :], self.p.device(axis, g))
+            return
+        self.coming[part, 1 + 3 * level].wait_recv()
+        self.coming[part, 3 + 3 * level].wait_recv()
+
+        def value(k):
+            return (self.keep[base + c * size + k, cells, :] + self.first[level][0, k, cells, :].astype(F32)
+                    + self.second[level][k, cells, :].astype(F32))
+        if level < 2:
+            self.halves(part, level + 1, value)
+        else:
+            self.total[cells, :] = value(0)
+
+    def finish(self):
+        for copy in self.sent:
+            copy.wait_send()
+
+    @staticmethod
+    def scratch():
+        vm = pltpu.VMEM
+        return [
+            vm((64, 256, 128), BF), vm((64, 256, 128), BF), vm((64, 256, 128), F32), vm((64, 256, 128), BF),
+            vm((2, 16, 256, 128), BF), vm((2, 4, 256, 128), BF), vm((2, 1, 256, 128), BF),
+            vm((16, 256, 128), BF), vm((4, 256, 128), BF), vm((1, 256, 128), BF),
+            vm((256, 128), F32),
+            pltpu.SemaphoreType.DMA((len(PARTS) * MOVES,)), pltpu.SemaphoreType.DMA((len(PARTS) * MOVES,)),
+            pltpu.SemaphoreType.DMA(()),
+        ]
+
+
+class Counts:
+    def __init__(self, place, own, held, got, send_sem, recv_sem):
+        self.p, self.held, self.got, self.send_sem, self.recv_sem = place, held, got, send_sem, recv_sem
+        held[0] = own[...]
+        self.partners = place.partners()
+        self.sent = []
+
+    def go(self, k):
+        copy = pltpu.make_async_remote_copy(
+            src_ref=self.held.at[k], dst_ref=self.got.at[k], send_sem=self.send_sem.at[k],
+            recv_sem=self.recv_sem.at[k], device_id=self.partners[k], device_id_type=MESH)
+        copy.start()
+        self.sent.append(copy)
+
+    def start(self):
+        self.go(0)
+
+    def round(self, k):
+        self.sent[k].wait_recv()
+        self.held[k + 1] = self.held[k] + self.got[k]
+        if k < 6:
+            self.go(k + 1)
+
+    def result(self):
+        return self.held[7]
+
+    def finish(self):
+        for copy in self.sent:
+            copy.wait_send()
+
+    @staticmethod
+    def scratch():
+        return [pltpu.VMEM((8, 8, 128), F32), pltpu.VMEM((7, 8, 128), F32),
+                pltpu.SemaphoreType.DMA((7,)), pltpu.SemaphoreType.DMA((7,))]
+
+
+class References:
+    def __init__(self, place, own, full, half, acc, zfirst, zsecond, pass_on, yown, ysend, ygot, send_sem, recv_sem):
+        self.p, self.own, self.full, self.half, self.acc = place, own, full, half, acc
+        self.zfirst, self.zsecond, self.pass_on = zfirst, zsecond, pass_on
+        self.yown, self.ysend, self.ygot = yown, ysend, ygot
+        self.send_sem, self.recv_sem = send_sem, recv_sem
+        self.sent, self.coming = [], {}
+        c = place.at[0]
+        self.c = c
+        self.f = (place.near[0], place.far[0])
+        self.g = (place.far[0], place.near[0])
+        self.h = place.cross[0]
+        self.ylo = place.at[1] % 2
+        self.lane = place.core * 2048
+
+    def move(self, s, k, src, dst, device):
+        copy = pltpu.make_async_remote_copy(
+            src_ref=src, dst_ref=dst, send_sem=self.send_sem.at[s * 10 + k], recv_sem=self.recv_sem.at[s * 10 + k],
+            device_id=device, device_id_type=MESH)
+        copy.start()
+        self.sent.append(copy)
+        self.coming[s, k] = copy
+
+    def lanes(self, at, size):
+        return pl.ds(pl.multiple_of(at, 256), size)
+
+    def share(self, s, k, at, size, device):
+        cells = self.full.at[s, :, self.lanes(at, size)]
+        self.move(s, k, cells, cells, device)
+
+    def start(self):
+        for s in range(2):
+            other = self.lanes((1 - self.p.core) * 2048, 2048)
+            self.move(s, 0, self.own.at[s, :, other], self.half.at[s], self.p.other_core())
+
+    def round(self, r):
+        for s in range(2):
+            self.step(r, s)
+
+    def step(self, r, s):
+        f, g, c, h = self.f[s], self.g[s], self.c, self.h
+        to_f, to_g = self.p.device(0, f), self.p.device(0, g)
+        to_y = self.p.device(1, self.p.near[1])
+        chunk = self.lane + c * 512
+        if r == 0:
+            self.coming[s, 0].wait_recv()
+            for k in range(4):
+                mine = self.own[s, :, self.lanes(self.lane + k * 512, 512)]
+                self.acc[s, k] = mine + self.half[s, :, k * 512:k * 512 + 512]
+            self.move(s, 2, self.acc.at[s, h], self.zfirst.at[s, 1], to_f)
+            self.move(s, 1, self.acc.at[s, f], self.zfirst.at[s, 0], to_f)
+        elif r == 1:
+            self.coming[s, 2].wait_recv()
+            self.pass_on[s] = self.acc[s, g] + self.zfirst[s, 1]
+            self.move(s, 3, self.pass_on.at[s], self.zsecond.at[s], to_g)
+        elif r == 2:
+            self.coming[s, 1].wait_recv()
+            self.coming[s, 3].wait_recv()
+            v = self.acc[s, c] + self.zfirst[s, 0] + self.zsecond[s]
+            low = self.ylo == 0
+            self.yown[s] = jnp.where(low, v[:, :256], v[:, 256:])
+            self.ysend[s] = jnp.where(low, v[:, 256:], v[:, :256])
+            self.move(s, 4, self.ysend.at[s], self.ygot.at[s], to_y)
+        elif r == 3:
+            self.coming[s, 4].wait_recv()
+            at = chunk + self.ylo * 256
+            self.full[s, :, self.lanes(at, 256)] = self.yown[s] + self.ygot[s]
+            self.share(s, 5, at, 256, to_y)
+        elif r == 4:
+            self.coming[s, 5].wait_recv()
+            self.share(s, 6, chunk, 512, to_g)
+        elif r == 5:
+            self.coming[s, 6].wait_recv()
+            self.share(s, 7, chunk, 512, to_f)
+            self.share(s, 8, self.lane + g * 512, 512, to_f)
+        elif r == 6:
+            self.coming[s, 7].wait_recv()
+            self.coming[s, 8].wait_recv()
+            self.share(s, 9, self.lane, 2048, self.p.other_core())
+        else:
+            self.coming[s, 9].wait_recv()
+
+    def finish(self):
+        for copy in self.sent:
+            copy.wait_send()
+
+    @staticmethod
+    def scratch():
+        vm = pltpu.VMEM
+        return [
+            vm((2, 64, 4096), BF), vm((2, 64, 2048), BF), vm((2, 4, 64, 512), BF), vm((2, 2, 64, 512), BF),
+            vm((2, 64, 512), BF), vm((2, 64, 512), BF), vm((2, 64, 256), BF), vm((2, 64, 256), BF), vm((2, 64, 256), BF),
+            pltpu.SemaphoreType.DMA((20,)), pltpu.SemaphoreType.DMA((20,)),
+        ]
+
+
+def average(total, counts, orient, out):
+    lane = lax.broadcasted_iota(jnp.int32, (8, 128), 1)
+    row = lax.broadcasted_iota(jnp.int32, (8, 128), 0)
+    count = jnp.sum(jnp.where((lane == orient) & (row == 0), counts, 0.0), keepdims=True)
+    for b in range(32):
+        out[0, :, b * 128:b * 128 + 128] = total[pl.ds(b, 8, stride=32), :] / count
+
+
+def exchange_kernel(own_refs, sums, counts, full_out, out, *scratch):
+    place = Place()
+    a, b, c = len(ClassSums.scratch()), len(Counts.scratch()), len(References.scratch())
+    s = scratch[:a]
+    classes = ClassSums(place, sums, s[0], s[1], s[2], s[3], s[4:7], s[7:10], s[10], s[11], s[12], s[13])
+    tally = Counts(place, counts, *scratch[a:a + b])
+    refs = References(place, own_refs, *scratch[a + b:a + b + c])
+    greet(place)
+    refs.start()
+    tally.start()
+    classes.start()
+    for r in range(8):
+        refs.round(r)
+        if r < 7:
+            tally.round(r)
+            classes.round(r)
+    full_out[...] = refs.full[...]
+    average(classes.total, tally.result(), lax.axis_index("orient"), out)
+    for part in (refs, tally, classes):
+        part.finish()
+
+
+def exchange_call(own_refs, sums, counts):
+    vm = pl.BlockSpec(memory_space=pltpu.VMEM)
+    return pl.pallas_call(
+        exchange_kernel,
+        out_shape=(jax.ShapeDtypeStruct((2, 64, 4096), BF), jax.ShapeDtypeStruct((1, 8, 4096), F32)),
+        in_specs=[vm, pl.BlockSpec(memory_space=pl.ANY), vm],
+        out_specs=(vm, vm),
+        scratch_shapes=ClassSums.scratch() + Counts.scratch() + References.scratch(),
+        compiler_params=pltpu.CompilerParams(
+            collective_id=0, has_side_effects=True, vmem_limit_bytes=56 * 2**20),
+    )(own_refs, sums.reshape(2, 64, 256, 128), counts)
+
+
 def local(subtomograms, rotated_refs, wedges, ref_pick, best_pick, class_of):
     orient_size, orient_index = lax.axis_size("orient"), lax.axis_index("orient")
     per = rotated_refs.shape[0]
@@ -376,16 +703,12 @@
             lax.dynamic_index_in_dim(rotated_refs, ref_pick[s] % per, 0, False), 0
         ) for s in range(STEPS)
     ]
-    refs = lax.psum(jnp.stack(mine), "orient")
     class_index = class_of[:, 0]
     sums = turn_call(subtomograms, best_pick, class_index)
-    received = lax.all_to_all(sums.reshape(CLASSES, 2048, 128), "orient", split_axis=0, concat_axis=0, tiled=True)
-    hits = class_index[None, :] == jnp.arange(CLASSES, dtype=jnp.int32)[:, None]
-    counts = lax.psum(jnp.sum(hits.astype(F32), axis=1), ("tomo", "orient"))
+    hits = class_index[None, :] == jnp.arange(128, dtype=jnp.int32)[:, None]
+    counts = jnp.broadcast_to(jnp.sum(hits.astype(F32), axis=1)[None], (8, 128))
+    refs, averages = exchange_call(jnp.stack(mine), sums, counts)
     result = scores_call(subtomograms, refs, wedge)
-    total = jnp.sum(received.astype(F32), axis=0).astype(BF)
-    slab = lax.psum_scatter(total, "tomo", scatter_dimension=0, tiled=True).astype(F32)
-    averages = (slab / lax.dynamic_index_in_dim(counts, orient_index, 0, False)).reshape(1, 8, 4096)
     return (result[:STEPS, :subtomograms.shape[0]], averages)
 
 

time: 300 us -> 122 us (0.41)
  blocking collectives: 161 us -> 0 us
  Pallas kernels: 57.2 us -> 107 us
  waiting for transfers between devices: 33.6 us -> 0 us
  between operations: 21 us -> 6.14 us
  starting transfers between devices: 7.04 us -> 0 us
  local copies, waits for them, and re-layouts: 11 us -> 4.51 us
  other arithmetic: 8.36 us -> 2.66 us
    psum x1 -> x0, blocking collectives: 161 us -> none  [local(): counts = lax.psum(jnp.sum(hits.astype(F32), axis=1), ('tomo', 'orient'))]
    pallas_call x0 -> x1, Pallas kernels: none -> 50.1 us  [exchange_call(): pl.pallas_call(exchange_kernel, out_shape=(jax.ShapeDtypeStruct((2, 64, 4...]
    reduce_scatter x1 -> x0, waiting for transfers between devices: 33.5 us -> none  [local(): lax.psum_scatter(total, 'tomo', scatter_dimension=0, tiled=True).astype(F32)]
    all_to_all x1 -> x0, starting transfers between devices: 6.96 us -> none  [local(): lax.all_to_all(sums.reshape(CLASSES, 2048, 128), 'orient', split_axis=0,...]
    unnamed x42 -> x39, local copies, waits for them, and re-layouts: 8.58 us -> 1.98 us
    reduce_sum x2 -> x1, other arithmetic: 5.7 us -> 0.08 us  [local(): counts = jnp.broadcast_to(jnp.sum(hits.astype(F32), axis=1)[None], (8, 128))]
  transfers between devices with their start and end apart: 3 -> 0, of which waited for: 1 -> 0; matrix products, arithmetic and copies ran while one was open for 3% -> 0% of each run, Pallas kernels for 11% -> 0%
where the time goes in v1:
time: 122 us; the launch traced here: 120 us
  Pallas kernels  107 us (88%)
  between operations  6.14 us (5%)
  local copies, waits for them, and re-layouts  4.51 us (4%)
  other arithmetic  2.66 us (2%)
    pallas_call x1, Pallas kernels, exchange_call(): pl.pallas_call(exchange_kernel, out_shape=(jax.ShapeDtypeStruct((2, 64, 4...  50.1 us
    pallas_call x1, Pallas kernels, scores_call(): pl.pallas_call(score_kernel, out_shape=jax.ShapeDtypeStruct((8, 128), F32...  33.9 us
    pallas_call x1, Pallas kernels, turn_call(): pl.pallas_call(turn_kernel, out_shape=jax.ShapeDtypeStruct((32768, 128),...  22.5 us

profile of v1, /device:TPU:0, one launch (start us, length us, event | category | flops | bytes accessed | tf_op | source)
XLA Modules:
  0.0 119.9 jit_solution(14372491897936670404)
XLA Ops:
  0.6 0.0 copy-start
  0.6 0.0 copy-start.14
  0.7 0.0 copy-start.4
  0.7 0.0 copy-start.15
  0.7 0.0 copy-start.12
  0.7 0.0 copy-start.5
  0.7 0.0 copy-start.17
  0.7 0.0 copy-start.16
  0.7 1.3 %fusion = (s32[1]{0:T(128)}, s32[1]{0:T(128)}) fusion(s32[2]{0:T(128)} %param.22), kind=kLoop, calls=%fused_computation.6 | loop fusion | bytes 16 | tf_op jit(solution)/shard_map/slice | solution.py:702
  7.3 0.0 copy-start.1
  7.3 1.4 %dynamic-slice_select_fusion.1 = (bf16[1,64,4096]{2,1,0:T(8,128)(2,1)S(1)}, bf16[1,64,4096]{2,1,0:T(8,128)(2,1)S(1)}) fusion(bf16[4,64,4096]{2,1,0:T(8,128)(2,1)} %param.20, s32[]{:T(128)S(6)} %select_n.51, pred[]{:T(512)S(6)} %eq.22, s32[]{:T(128)S(6)} %select_n.56, pred[]{:T(512)S(6)} %eq.23), kind=kLoop, calls=%fused_computation.3 | loop fusion | flops 524288 | bytes 2097162 | tf_op jit(solution)/shard_map/jit(_where)/select_n | solution.py:701
  8.7 1.2 pad_maximum_fusion.own_refs
  9.9 0.0 copy-done.14
  9.9 0.0 copy-done.4
  9.9 0.0 copy-done.15
  9.9 0.0 copy-done.12
  9.9 0.0 copy-done.5
  9.9 0.0 copy-done.17
  9.9 0.0 copy-done.16
  9.9 0.0 copy-done.1
  9.9 22.5 %shard_map.194 = bf16[32768,128]{1,0:T(8,128)(2,1)} custom-call(s32[6]{0:T(128)S(1)} %copy-done.16, s32[6]{0:T(128)S(1)} %bitcast.6, bf16[6,64,4096]{2,1,0:T(8,128)(2,1)S(1)} %copy-done.1, bf16[64,128]{1,0:T(8,128)(2,1)S(1)} %copy-done.14, bf16[256,256]{1,0:T(8,128)(2,1)S(1)} %copy-done.4, bf16[64,64]{1,0:T(8,128)(2,1)S(1)} %copy-done.15, ...), custom_call_target="tpu_custom_call" | custom-call | tf_op jit(solution)/shard_map/pallas_call | solution.py:359
  32.5 0.1 convert_reduce_fusion
  32.5 0.6 broadcast_in_dim.13.counts
  33.1 0.0 copy-start.2
  33.1 0.0 copy-start.6
  33.1 0.0 copy-start.7
  33.1 0.0 copy-start.8
  33.1 0.0 copy-start.9
  33.2 0.0 copy-start.10
  33.2 0.0 copy-start.11
  33.2 0.0 copy-start.13
  33.2 50.1 %shard_map.195 = (bf16[2,64,4096]{2,1,0:T(8,128)(2,1)}, f32[1,8,4096]{2,1,0:T(8,128)}) custom-call(bf16[2,64,4096]{2,1,0:T(8,128)(2,1)} %pad_maximum_fusion.own_refs, bf16[2,64,256,128]{3,2,1,0:T(8,128)(2,1)} %bitcast.8, f32[8,128]{1,0:T(8,128)} %broadcast_in_dim.13.counts), custom_call_target="tpu_custom_call" | custom-call | tf_op jit(solution)/shard_map/pallas_call | solution.py:685
  83.4 0.0 copy-done
  83.4 0.0 copy-done.2
  83.4 0.0 copy-done.6
  83.4 0.0 copy-done.7
  83.4 0.0 copy-done.8
  83.5 0.0 copy-done.9
  83.5 0.0 copy-done.10
  83.5 0.0 copy-done.11
  83.5 0.0 copy-done.13
  83.5 0.0 copy-start.3
  83.5 1.2 %copy-done.3 = bf16[2,64,4096]{2,1,0:T(8,128)(2,1)S(1)} copy-done((bf16[2,64,4096]{2,1,0:T(8,128)(2,1)S(1)}, bf16[2,64,4096]{2,1,0:T(8,128)(2,1)}, u32[]{:S(2)}) %copy-start.3) | copy-done | bytes 1048600
  84.7 0.0 copy-start.18
  84.7 33.9 %shard_map.196 = f32[8,128]{1,0:T(8,128)S(1)} custom-call(bf16[6,64,4096]{2,1,0:T(8,128)(2,1)} %v.3, bf16[2,64,4096]{2,1,0:T(8,128)(2,1)S(1)} %copy-done.3, bf16[64,4096]{1,0:T(8,128)(2,1)S(1)} %dynamic-slice_bitcast_fusion.wedge, bf16[2,64,64]{2,1,0:T(8,128)(2,1)S(1)} %copy-done.11, bf16[2,512,512]{2,1,0:T(8,128)(2,1)S(1)} %copy-done.2, ...), custom_call_target="tpu_custom_call" | custom-call | tf_op jit(solution)/shard_map/pallas_call | solution.py:231
  118.6 0.6 slice.13
  119.2 0.0 copy-done.18
  119.2 0.7 copy.22
  (1 shorter events, 0.0 us)
Async XLA Ops:
  0.6 82.7 %copy-start = (bf16[2,64,4096]{2,1,0:T(8,128)(2,1)S(1)}, bf16[2,64,4096]{2,1,0:T(8,128)(2,1)}, u32[]{:S(2)}) copy-start(bf16[2,64,4096]{2,1,0:T(8,128)(2,1)} %param.21) | copy-start | bytes 3145732
  0.6 9.2 %copy-start.14 = (bf16[64,128]{1,0:T(8,128)(2,1)S(1)}, bf16[64,128]{1,0:T(8,128)(2,1)}, u32[]{:S(2)}) copy-start(bf16[64,128]{1,0:T(8,128)(2,1)} %constant.93.clone.pair) | copy-start | bytes 49156
  0.7 9.2 %copy-start.4 = (bf16[256,256]{1,0:T(8,128)(2,1)S(1)}, bf16[256,256]{1,0:T(8,128)(2,1)}, u32[]{:S(2)}) copy-start(bf16[256,256]{1,0:T(8,128)(2,1)} %constant.94.clone.lanes) | copy-start | bytes 393220
  0.7 9.2 %copy-start.15 = (bf16[64,64]{1,0:T(8,128)(2,1)S(1)}, bf16[64,64]{1,0:T(8,128)(2,1)}, u32[]{:S(2)}) copy-start(bf16[64,64]{1,0:T(8,128)(2,1)} %constant.95.clone.rows) | copy-start | bytes 24580
  0.7 9.2 %copy-start.12 = (bf16[2,64,64]{2,1,0:T(8,128)(2,1)S(1)}, bf16[2,64,64]{2,1,0:T(8,128)(2,1)}, u32[]{:S(2)}) copy-start(bf16[2,64,64]{2,1,0:T(8,128)(2,1)} %constant.96.clone.flip_rows) | copy-start | bytes 49156
  0.7 9.2 %copy-start.5 = (bf16[4,128,128]{2,1,0:T(8,128)(2,1)S(1)}, bf16[4,128,128]{2,1,0:T(8,128)(2,1)}, u32[]{:S(2)}) copy-start(bf16[4,128,128]{2,1,0:T(8,128)(2,1)} %constant.97.clone.flip_lanes) | copy-start | bytes 393220
  0.7 9.2 %copy-start.17 = (s32[6,1]{0,1:T(1,128)S(1)}, s32[6,1]{0,1:T(1,128)}, u32[]{:S(2)}) copy-start(s32[6,1]{0,1:T(1,128)} %param.24) | copy-start | bytes 76
  0.7 9.2 %copy-start.16 = (s32[6]{0:T(128)S(1)}, s32[6]{0:T(128)}, u32[]{:S(2)}) copy-start(s32[6]{0:T(128)} %pick.1) | copy-start | bytes 76
  7.3 2.6 %copy-start.1 = (bf16[6,64,4096]{2,1,0:T(8,128)(2,1)S(1)}, bf16[6,64,4096]{2,1,0:T(8,128)(2,1)}, u32[]{:S(2)}) copy-start(bf16[6,64,4096]{2,1,0:T(8,128)(2,1)} %v.3) | copy-start | bytes 9437188
  33.1 50.3 %copy-start.2 = (bf16[2,512,512]{2,1,0:T(8,128)(2,1)S(1)}, bf16[2,512,512]{2,1,0:T(8,128)(2,1)}, u32[]{:S(2)}) copy-start(bf16[2,512,512]{2,1,0:T(8,128)(2,1)} %constant.99.clone.tzf) | copy-start | bytes 3145732
  33.1 50.3 %copy-start.6 = (bf16[256,256]{1,0:T(8,128)(2,1)S(1)}, bf16[256,256]{1,0:T(8,128)(2,1)}, u32[]{:S(2)}) copy-start(bf16[256,256]{1,0:T(8,128)(2,1)} %constant.102.clone.tzi) | copy-start | bytes 393220
  33.1 50.3 %copy-start.7 = (bf16[2,128,128]{2,1,0:T(8,128)(2,1)S(1)}, bf16[2,128,128]{2,1,0:T(8,128)(2,1)}, u32[]{:S(2)}) copy-start(bf16[2,128,128]{2,1,0:T(8,128)(2,1)} %constant.100.clone.tyf) | copy-start | bytes 196612
  33.1 50.3 %copy-start.8 = (bf16[128,128]{1,0:T(8,128)(2,1)S(1)}, bf16[128,128]{1,0:T(8,128)(2,1)}, u32[]{:S(2)}) copy-start(bf16[128,128]{1,0:T(8,128)(2,1)} %constant.101.clone.tyi) | copy-start | bytes 98308
  33.1 50.3 %copy-start.9 = (bf16[128,128]{1,0:T(8,128)(2,1)S(1)}, bf16[128,128]{1,0:T(8,128)(2,1)}, u32[]{:S(2)}) copy-start(bf16[128,128]{1,0:T(8,128)(2,1)} %constant.104.clone.fr) | copy-start | bytes 98308
  33.2 50.3 %copy-start.10 = (bf16[128,128]{1,0:T(8,128)(2,1)S(1)}, bf16[128,128]{1,0:T(8,128)(2,1)}, u32[]{:S(2)}) copy-start(bf16[128,128]{1,0:T(8,128)(2,1)} %constant.105.clone.fl) | copy-start | bytes 98308
  33.2 50.3 %copy-start.11 = (bf16[2,64,64]{2,1,0:T(8,128)(2,1)S(1)}, bf16[2,64,64]{2,1,0:T(8,128)(2,1)}, u32[]{:S(2)}) copy-start(bf16[2,64,64]{2,1,0:T(8,128)(2,1)} %constant.98.clone.txf) | copy-start | bytes 49156
  33.2 50.3 %copy-start.13 = (bf16[64,64]{1,0:T(8,128)(2,1)S(1)}, bf16[64,64]{1,0:T(8,128)(2,1)}, u32[]{:S(2)}) copy-start(bf16[64,64]{1,0:T(8,128)(2,1)} %constant.103.clone.txi) | copy-start | bytes 24580
  83.5 1.2 %copy-start.3 = (bf16[2,64,4096]{2,1,0:T(8,128)(2,1)S(1)}, bf16[2,64,4096]{2,1,0:T(8,128)(2,1)}, u32[]{:S(2)}) copy-start(bf16[2,64,4096]{2,1,0:T(8,128)(2,1)} %get-tuple-element.4.refs) | copy-start | bytes 3145732
  84.7 34.5 %copy-start.18 = (f32[1,8,4096]{2,1,0:T(8,128)S(1)}, f32[1,8,4096]{2,1,0:T(8,128)}, u32[]{:S(2)}) copy-start(f32[1,8,4096]{2,1,0:T(8,128)} %get-tuple-element.13) | copy-start | bytes 393220

commit v2 on v1

--- a/solution.py
+++ b/solution.py
@@ -14,6 +14,10 @@
 BF = jnp.bfloat16
 F32 = jnp.float32
 MESH = pl.DeviceIdType.MESH
+PITCH_FWD = 36
+PITCH_INV = 68
+PITCH_WIDE = 68
+PITCH_TOTAL = 36
 
 
 def score_tables():
@@ -60,29 +64,34 @@
     return jnp.dot(a, b, preferred_element_type=F32)
 
 
-def forward(first, second, tx, tz, ty, left, plane, out):
-    for q, vol in enumerate((first, second)):
-        def x_pass(c, _):
-            at = pl.multiple_of(c * 512, 512)
-            r = dot(tx, vol[:, pl.ds(at, 512)]).astype(BF)
-            for k in range(4):
-                rows = pl.ds(pl.multiple_of((c * 4 + k) * 32, 32), 32)
-                left[rows, q * 256:q * 256 + 128] = r[:32, k * 128:k * 128 + 128]
-                left[rows, q * 256 + 128:q * 256 + 256] = r[32:, k * 128:k * 128 + 128]
-            return 0
-        lax.fori_loop(0, 8, x_pass, 0, unroll=8)
-
+def forward_x(vol, q, tx, left):
+    def x_pass(c, _):
+        at = pl.multiple_of(c * 512, 512)
+        r = dot(tx, vol[:, pl.ds(at, 512)]).astype(BF)
+        for k in range(4):
+            rows = pl.ds(pl.multiple_of((c * 4 + k) * 32, 32), 32)
+            left[rows, q * 256:q * 256 + 128] = r[:32, k * 128:k * 128 + 128]
+            left[rows, q * 256 + 128:q * 256 + 256] = r[32:, k * 128:k * 128 + 128]
+        return 0
+    lax.fori_loop(0, 8, x_pass, 0, unroll=8)
+
+
+def forward_z(tz, left, plane):
     def z_pass(m, _):
         at = pl.multiple_of(m * 128, 128)
         r = dot(left[pl.ds(at, 128), :], tz)
         for col in range(4):
-            plane[pl.ds(col * 1024 + at, 128), :] = r[:, col * 128:col * 128 + 128]
+            for k in range(4):
+                row = (col * 32 + m * 4 + k) * PITCH_FWD
+                plane[pl.ds(row, 32), :] = r[k * 32:k * 32 + 32, col * 128:col * 128 + 128]
         return 0
     lax.fori_loop(0, 8, z_pass, 0, unroll=8)
 
+
+def forward_y(ty, plane, out):
     def y_pass(m, _):
         d = jnp.concatenate(
-            [plane[pl.ds(2 * m + k, 128, stride=32), :] for k in range(2)], 1).astype(BF)
+            [plane[pl.ds(2 * m + k, 128, stride=PITCH_FWD), :] for k in range(2)], 1).astype(BF)
         r = dot(ty, d).astype(BF)
         for k in range(2):
             out[pl.ds(pl.multiple_of((2 * m + k) * 128, 128), 128), :] = r[:, k * 128:k * 128 + 128]
@@ -152,7 +161,7 @@
     lax.fori_loop(1, 32, body, 0)
 
 
-def correlate(spec, twin, filt, extra, ty, tz, tx, left, plane):
+def correlate_y(spec, twin, filt, extra, ty, left):
     def times(v, w):
         return (v[:64] * w[:64] - v[64:] * w[64:], v[:64] * w[64:] + v[64:] * w[:64])
 
@@ -176,71 +185,27 @@
         return 0
     lax.fori_loop(1, 16, y_pass, 0, unroll=15)
 
+
+def correlate_z(tz, left, plane):
     def z_pass(m, _):
         at = pl.multiple_of(m * 256, 256)
         r = dot(left[pl.ds(at, 256), 0:256], tz)
         for p in range(2):
-            plane[pl.ds(p * 2048 + at, 256), :] = r[:, p * 128:p * 128 + 128]
+            for k in range(4):
+                row = (p * 32 + m * 4 + k) * PITCH_INV
+                plane[pl.ds(row, 64), :] = r[k * 64:k * 64 + 64, p * 128:p * 128 + 128]
         return 0
     lax.fori_loop(0, 8, z_pass, 0, unroll=8)
 
+
+def correlate_x(tx, plane):
     def x_pass(m, top):
         d = jnp.concatenate(
-            [plane[pl.ds(2 * m + k, 64, stride=64), :] for k in range(2)], 1).astype(BF)
+            [plane[pl.ds(2 * m + k, 64, stride=PITCH_INV), :] for k in range(2)], 1).astype(BF)
         r = dot(tx, d)
         return jnp.maximum(top, jnp.maximum(r[:, :128], r[:, 128:]))
     top = lax.fori_loop(0, 32, x_pass, jnp.full((64, 128), -jnp.inf, F32), unroll=16)
     return functools.reduce(jnp.maximum, [top[8 * k:8 * k + 8] for k in range(8)])
-
-
-def score_kernel(v, refs, wedge, txf, tzf, tyf, tyi, tzi, txi, fr, fl, out,
-                 left, plane, spec, rspec, twin, weight, edge, filt, extra):
-    low = lax.broadcasted_iota(jnp.int32, (64, 128), 1) < 64
-    low8 = low[:8]
-
-    def halves(t, op, fill):
-        f = jnp.max if op == "max" else jnp.sum
-        return [f(jnp.where(low8 == (k == 0), t, fill), keepdims=True) for k in range(2)]
-
-    forward(wedge, wedge, txf[1], tzf[1], tyf[1], left, plane, rspec)
-    wedge_setup(rspec, fr[...], fl[...], weight, edge)
-    forward(refs.at[0], refs.at[1], txf[0], tzf[0], tyf[0], left, plane, rspec)
-    rt = mirror(rspec[0:128, :], fr[...], fl[...])
-    rp = halves(power(rspec, rt, weight, edge), "sum", 0.0)
-    reference_setup(rspec, rt, weight, edge, low, filt, extra)
-    row = lax.broadcasted_iota(jnp.int32, (8, 128), 0)
-    lane = lax.broadcasted_iota(jnp.int32, (8, 128), 1)
-
-    def one_pair(pair, result):
-        forward(v.at[2 * pair], v.at[2 * pair + 1], txf[0], tzf[0], tyf[0], left, plane, spec)
-        t = mirror(spec[0:128, :], fr[...], fl[...])
-        own = halves(power(spec, t, weight, edge), "sum", 0.0)
-
-        def one_step(s, result):
-            top = halves(correlate(spec, t, filt.at[s], extra[s], tyi[...], tzi[...], txi[...], left, plane), "max", -jnp.inf)
-            for k in range(2):
-                norm = jnp.sqrt(own[k] * jnp.where(s == 0, rp[0], rp[1]) / float(N ** 3) + 1e-6)
-                result = jnp.where((row == s) & (lane == 2 * pair + k), top[k] / norm, result)
-            return result
-        return lax.fori_loop(0, 2, one_step, result)
-    out[...] = lax.fori_loop(0, 3, one_pair, jnp.zeros((8, 128), F32))
-
-
-def scores_call(v, refs, wedge):
-    tables = [jnp.asarray(t, dtype=BF) for t in score_tables()]
-    return pl.pallas_call(
-        score_kernel,
-        out_shape=jax.ShapeDtypeStruct((8, 128), F32),
-        in_specs=[pl.BlockSpec(memory_space=pltpu.VMEM)] * 11,
-        out_specs=pl.BlockSpec(memory_space=pltpu.VMEM),
-        scratch_shapes=[
-            pltpu.VMEM((2048, 512), BF), pltpu.VMEM((4096, 128), F32),
-            pltpu.VMEM((4096, 128), BF), pltpu.VMEM((4096, 128), BF),
-            pltpu.VMEM((128, 128), F32), pltpu.VMEM((2048, 128), F32), pltpu.VMEM((128, 128), F32),
-            pltpu.VMEM((2, 4096, 128), F32), pltpu.VMEM((2, 128, 128), F32),
-        ],
-        compiler_params=pltpu.CompilerParams(vmem_limit_bytes=50 * 2**20),
-    )(v, refs, wedge, *tables)
 
 
 def turn_tables():
@@ -254,13 +219,40 @@
     return [pair, lanes, rows, flip_rows, flip_lanes]
 
 
-def turn_kernel(pick, classes, v, pair, lanes, rows, flip_rows, flip_lanes, out, held, wide, mixed, sums):
+def turn_kernel(ref_pick, pick, classes, refs, v, pair, lanes, rows, flip_rows, flip_lanes,
+                out, own_refs, counts, held, wide, mixed, total, narrow, empty, out_sem, ref_sem):
     low = lax.broadcasted_iota(jnp.int32, (64, 128), 1) < 64
-
-    def clear(k, _):
-        sums[pl.ds(pl.multiple_of(k * 512, 512), 512), :] = jnp.zeros((512, 128), F32)
-        return 0
-    lax.fori_loop(0, 64, clear, 0)
+    me, per = lax.axis_index("orient"), refs.shape[0]
+
+    def fetch(s):
+        return pltpu.make_async_copy(refs.at[ref_pick[s] % per], own_refs.at[s], ref_sem.at[s])
+
+    for s in range(2):
+        @pl.when(ref_pick[s] // per == me)
+        def _():
+            fetch(s).start()
+
+        @pl.when(ref_pick[s] // per != me)
+        def _():
+            own_refs[s] = jnp.zeros(own_refs.shape[1:], BF)
+
+    def store(c, src):
+        return pltpu.make_async_copy(src, out.at[c % 2, c // 2], out_sem.at[c])
+
+    empty[...] = jnp.zeros(empty.shape, BF)
+    lane = lax.broadcasted_iota(jnp.int32, (8, 128), 1)
+    tally = jnp.zeros((8, 128), F32)
+    for i in range(6):
+        tally = tally + (lane == classes[i]).astype(F32)
+    counts[...] = tally
+    for c in range(CLASSES):
+        hit = classes[0] == c
+        for i in range(1, 6):
+            hit = hit | (classes[i] == c)
+
+        @pl.when(jnp.logical_not(hit))
+        def _():
+            store(c, empty).start()
 
     def swap_ends():
         def body(m, _):
@@ -277,13 +269,15 @@
 
     def swap_first():
         def widen(m, _):
-            at = pl.ds(pl.multiple_of(m * 256, 256), 256)
-            wide[at, :] = held[at, :].astype(F32)
+            for k in range(4):
+                b = m * 4 + k
+                blk = held[pl.ds(pl.multiple_of(b * 64, 64), 64), :]
+                wide[pl.ds(b * PITCH_WIDE, 64), :] = blk.astype(F32)
             return 0
         lax.fori_loop(0, 8, widen, 0, unroll=8)
 
         def gather(m, _):
-            d = [wide[pl.ds(2 * m + k, 32, stride=64), :] for k in range(2)]
+            d = [wide[pl.ds(2 * m + k, 32, stride=PITCH_WIDE), :] for k in range(2)]
             mixed[pl.ds(pl.multiple_of(m * 32, 32), 32), :] = jnp.concatenate(d, 1).astype(BF)
             return 0
         lax.fori_loop(0, 32, gather, 0, unroll=32)
@@ -298,7 +292,7 @@
             return 0
         lax.fori_loop(0, 4, body, 0, unroll=4)
 
-    def one(i, _):
+    def turn(i, first):
         number = pick[i]
         order, place = number // 4, number % 4
         even = (order == 0) | (order == 3) | (order == 4)
@@ -310,8 +304,6 @@
         pl.when((order == 1) | (order == 3) | (order == 5))(swap_ends)
         pl.when((order >= 1) & (order <= 4))(swap_first)
         pl.when((order == 1) | (order == 4))(swap_ends)
-        c = classes[i]
-        base = ((c % 2) * 8 + c // 2) * 2048
         j0, jl = flip_rows[f0], flip_lanes[f1 * 2 + f2]
 
         def flip_ends(m, _):
@@ -333,8 +325,9 @@
                 u = dot(j0, jnp.concatenate(blocks, 1))
                 blocks = [u[:, k * 128:k * 128 + 128] for k in range(4)]
             for k in range(4):
-                at = pl.ds(base + m * 4 + k, 64, stride=32)
-                sums[at, :] = sums[at, :] + blocks[k].astype(F32)
+                at = pl.ds(m * 4 + k, 64, stride=PITCH_TOTAL)
+                u = blocks[k].astype(F32)
+                total[at, :] = u if first else total[at, :] + u
 
         @pl.when(f0 > 0)
         def _():
@@ -343,27 +336,61 @@
         @pl.when(f0 == 0)
         def _():
             lax.fori_loop(0, 8, lambda m, c: (add(m, False), c)[1], 0, unroll=8)
+
+    def one(i, _):
+        c = classes[i]
+
+        def count(j, n):
+            return n + (classes[j] == c).astype(jnp.int32)
+
+        @pl.when(lax.fori_loop(0, i, count, 0) == 0)
+        def _():
+            turn(i, True)
+
+            def later(j, _):
+                @pl.when(classes[j] == c)
+                def _():
+                    turn(j, False)
+                return 0
+            lax.fori_loop(i + 1, 6, later, 0)
+
+            def shorten(k, _):
+                for d in range(8):
+                    at = pl.ds(pl.multiple_of(k * 256 + d * 32, 32), 32)
+                    narrow[i, at, :] = total[pl.ds((k * 8 + d) * PITCH_TOTAL, 32), :].astype(BF)
+                return 0
+            lax.fori_loop(0, 8, shorten, 0, unroll=8)
+            store(c, narrow.at[i]).start()
         return 0
     lax.fori_loop(0, 6, one, 0)
 
-    def narrow(k, _):
-        at = pl.ds(pl.multiple_of(k * 512, 512), 512)
-        out[at, :] = sums[at, :].astype(BF)
-        return 0
-    lax.fori_loop(0, 64, narrow, 0)
-
-
-def turn_call(v, pick, classes):
+    for s in range(2):
+        @pl.when(ref_pick[s] // per == me)
+        def _():
+            fetch(s).wait()
+    for c in range(CLASSES):
+        store(c, empty).wait()
+
+
+def turn_call(ref_pick, pick, classes, refs, v):
     tables = [jnp.asarray(t, dtype=BF) for t in turn_tables()]
-    vm = pl.BlockSpec(memory_space=pltpu.VMEM)
+    sm, vm, far = [pl.BlockSpec(memory_space=m) for m in (pltpu.SMEM, pltpu.VMEM, pl.ANY)]
     return pl.pallas_call(
         turn_kernel,
-        out_shape=jax.ShapeDtypeStruct((32768, 128), BF),
-        in_specs=[pl.BlockSpec(memory_space=pltpu.SMEM)] * 2 + [vm] * 6,
-        out_specs=vm,
-        scratch_shapes=[pltpu.VMEM((2048, 128), BF), pltpu.VMEM((2048, 128), F32), pltpu.VMEM((1024, 256), BF), pltpu.VMEM((32768, 128), F32)],
-        compiler_params=pltpu.CompilerParams(vmem_limit_bytes=50 * 2**20),
-    )(pick, classes, v, *tables)
+        out_shape=(
+            jax.ShapeDtypeStruct((2, 8, 2048, 128), BF),
+            jax.ShapeDtypeStruct((2,) + refs.shape[1:], BF),
+            jax.ShapeDtypeStruct((8, 128), F32),
+        ),
+        in_specs=[sm] * 3 + [far] + [vm] * 6,
+        out_specs=(far, vm, vm),
+        scratch_shapes=[
+            pltpu.VMEM((2048, 128), BF), pltpu.VMEM((2304, 128), F32), pltpu.VMEM((1024, 256), BF),
+            pltpu.VMEM((2560, 128), F32), pltpu.VMEM((6, 2048, 128), BF), pltpu.VMEM((2048, 128), BF),
+            pltpu.SemaphoreType.DMA((CLASSES,)), pltpu.SemaphoreType.DMA((2,)),
+        ],
+        compiler_params=pltpu.CompilerParams(vmem_limit_bytes=40 * 2**20),
+    )(ref_pick, pick, classes, refs, v, *tables)
 
 
 PARTS = (
@@ -658,58 +685,142 @@
         out[0, :, b * 128:b * 128 + 128] = total[pl.ds(b, 8, stride=32), :] / count
 
 
-def exchange_kernel(own_refs, sums, counts, full_out, out, *scratch):
+class Scores:
+    def __init__(self, v, wedge, full, tables, out, scratch):
+        self.v, self.wedge, self.full, self.out = v, wedge, full, out
+        self.txf, self.tzf, self.tyf, self.tyi, self.tzi, self.txi, self.fr, self.fl = tables
+        self.left, self.plane, self.spec, self.rspec, self.weight, self.edge, self.filt, self.extra = scratch
+        self.low = lax.broadcasted_iota(jnp.int32, (64, 128), 1) < 64
+        self.row = lax.broadcasted_iota(jnp.int32, (8, 128), 0)
+        self.lane = lax.broadcasted_iota(jnp.int32, (8, 128), 1)
+        self.result = jnp.zeros((8, 128), F32)
+        self.twin, self.own = {}, {}
+
+    def halves(self, t, op, fill):
+        return [op(jnp.where(self.low[:8] == (k == 0), t, fill), keepdims=True) for k in range(2)]
+
+    def forward(self, first, second, kind, out):
+        def x():
+            forward_x(first, 0, self.txf[kind], self.left)
+            forward_x(second, 1, self.txf[kind], self.left)
+        return [
+            (0.6, x),
+            (0.9, lambda: forward_z(self.tzf[kind], self.left, self.plane)),
+            (0.6, lambda: forward_y(self.tyf[kind], self.plane, out)),
+        ]
+
+    def mirror(self, spec):
+        return mirror(spec[0:128, :], self.fr[...], self.fl[...])
+
+    def wedge_work(self):
+        return self.forward(self.wedge, self.wedge, 1, self.rspec) + [
+            (0.2, lambda: wedge_setup(self.rspec, self.fr[...], self.fl[...], self.weight, self.edge))]
+
+    def pair_work(self, pair):
+        spec = self.spec.at[pair]
+
+        def after():
+            self.twin[pair] = self.mirror(spec)
+            self.own[pair] = self.halves(power(spec, self.twin[pair], self.weight, self.edge), jnp.sum, 0.0)
+        return self.forward(self.v.at[2 * pair], self.v.at[2 * pair + 1], 0, spec) + [(0.3, after)]
+
+    def reference_work(self):
+        def after():
+            t = self.mirror(self.rspec)
+            self.norm = self.halves(power(self.rspec, t, self.weight, self.edge), jnp.sum, 0.0)
+            reference_setup(self.rspec, t, self.weight, self.edge, self.low, self.filt, self.extra)
+        return self.forward(self.full.at[0], self.full.at[1], 0, self.rspec) + [(0.7, after)]
+
+    def score_work(self, pair, s):
+        def last():
+            top = self.halves(correlate_x(self.txi[...], self.plane), jnp.max, -jnp.inf)
+            for k in range(2):
+                score = top[k] / jnp.sqrt(self.own[pair][k] * self.norm[s] / float(N ** 3) + 1e-6)
+                self.result = jnp.where((self.row == s) & (self.lane == 2 * pair + k), score, self.result)
+        return [
+            (1.0, lambda: correlate_y(self.spec.at[pair], self.twin[pair], self.filt.at[s], self.extra[s],
+                                      self.tyi[...], self.left)),
+            (0.6, lambda: correlate_z(self.tzi[...], self.left, self.plane)),
+            (0.8, last),
+        ]
+
+    def finish(self):
+        self.out[...] = self.result[:self.out.shape[0], :self.out.shape[1]]
+
+    @staticmethod
+    def scratch():
+        vm = pltpu.VMEM
+        return [
+            vm((2048, 512), BF), vm((4608, 128), F32), vm((3, 4096, 128), BF), vm((4096, 128), BF),
+            vm((2048, 128), F32), vm((128, 128), F32), vm((2, 4096, 128), F32), vm((2, 128, 128), F32),
+        ]
+
+
+def interleave(work, events):
+    events = sorted(events, key=lambda e: e[0])
+    clock = 0.0
+    for length, piece in work:
+        while events and events[0][0] <= clock:
+            events.pop(0)[1]()
+        piece()
+        clock += length
+    for _, action in events:
+        action()
+
+
+REF_TIMES = (1.5, 2.4, 3.3, 4.2, 5.4, 6.3, 7.5, 9.2)
+CLASS_TIMES = ((2.2, 1.2), (10.0, 1.0), (16.0, 0.8), (21.0, 0.4), (24.0, 0.3), (26.0, 0.3), (28.0, 0.2))
+
+
+def fused_kernel(own_refs, sums, counts, v, wedges, *rest):
+    tables, (scores_out, out), scratch = rest[:8], rest[8:10], rest[10:]
     place = Place()
-    a, b, c = len(ClassSums.scratch()), len(Counts.scratch()), len(References.scratch())
-    s = scratch[:a]
+    ends = np.cumsum([0] + [len(c.scratch()) for c in (ClassSums, Counts, References, Scores)])
+    s, tally_s, refs_s, score_s = [scratch[i:j] for i, j in zip(ends, ends[1:])]
     classes = ClassSums(place, sums, s[0], s[1], s[2], s[3], s[4:7], s[7:10], s[10], s[11], s[12], s[13])
-    tally = Counts(place, counts, *scratch[a:a + b])
-    refs = References(place, own_refs, *scratch[a + b:a + b + c])
+    tally = Counts(place, counts, *tally_s)
+    refs = References(place, own_refs, *refs_s)
+    orient = lax.axis_index("orient")
+    scores = Scores(v, wedges.at[orient * wedges.shape[0] // lax.axis_size("orient")], refs.full, tables, scores_out, score_s)
     greet(place)
     refs.start()
     tally.start()
     classes.start()
-    for r in range(8):
-        refs.round(r)
-        if r < 7:
-            tally.round(r)
-            classes.round(r)
-    full_out[...] = refs.full[...]
-    average(classes.total, tally.result(), lax.axis_index("orient"), out)
+    events = [(t, functools.partial(refs.round, r)) for r, t in enumerate(REF_TIMES)]
+    for r, (t, gap) in enumerate(CLASS_TIMES):
+        events += [(t + gap * part, functools.partial(classes.step, r, part)) for part in range(len(PARTS))]
+        events.append((t + gap * len(PARTS), functools.partial(tally.round, r)))
+    work = scores.wedge_work()
+    for pair in range(3):
+        work += scores.pair_work(pair)
+    work += scores.reference_work()
+    for pair in range(3):
+        for step in range(STEPS):
+            work += scores.score_work(pair, step)
+    interleave(work, events)
+    scores.finish()
+    average(classes.total, tally.result(), orient, out)
     for part in (refs, tally, classes):
         part.finish()
 
 
-def exchange_call(own_refs, sums, counts):
+def fused_call(own_refs, sums, counts, v, wedges):
+    tables = [jnp.asarray(t, dtype=BF) for t in score_tables()]
     vm = pl.BlockSpec(memory_space=pltpu.VMEM)
     return pl.pallas_call(
-        exchange_kernel,
-        out_shape=(jax.ShapeDtypeStruct((2, 64, 4096), BF), jax.ShapeDtypeStruct((1, 8, 4096), F32)),
-        in_specs=[vm, pl.BlockSpec(memory_space=pl.ANY), vm],
+        fused_kernel,
+        out_shape=(jax.ShapeDtypeStruct((STEPS, v.shape[0]), F32), jax.ShapeDtypeStruct((1, 8, 4096), F32)),
+        in_specs=[vm, pl.BlockSpec(memory_space=pl.ANY)] + [vm] * 11,
         out_specs=(vm, vm),
-        scratch_shapes=ClassSums.scratch() + Counts.scratch() + References.scratch(),
+        scratch_shapes=sum([c.scratch() for c in (ClassSums, Counts, References, Scores)], []),
         compiler_params=pltpu.CompilerParams(
-            collective_id=0, has_side_effects=True, vmem_limit_bytes=56 * 2**20),
-    )(own_refs, sums.reshape(2, 64, 256, 128), counts)
+            collective_id=0, has_side_effects=True, vmem_limit_bytes=60 * 2**20),
+    )(own_refs, sums.reshape(2, 64, 256, 128), counts, v, wedges, *tables)
 
 
 def local(subtomograms, rotated_refs, wedges, ref_pick, best_pick, class_of):
-    orient_size, orient_index = lax.axis_size("orient"), lax.axis_index("orient")
-    per = rotated_refs.shape[0]
-    wedge = lax.dynamic_index_in_dim(wedges, orient_index * wedges.shape[0] // orient_size, 0, False)
-    mine = [
-        jnp.where(
-            ref_pick[s] // per == orient_index,
-            lax.dynamic_index_in_dim(rotated_refs, ref_pick[s] % per, 0, False), 0
-        ) for s in range(STEPS)
-    ]
-    class_index = class_of[:, 0]
-    sums = turn_call(subtomograms, best_pick, class_index)
-    hits = class_index[None, :] == jnp.arange(128, dtype=jnp.int32)[:, None]
-    counts = jnp.broadcast_to(jnp.sum(hits.astype(F32), axis=1)[None], (8, 128))
-    refs, averages = exchange_call(jnp.stack(mine), sums, counts)
-    result = scores_call(subtomograms, refs, wedge)
-    return (result[:STEPS, :subtomograms.shape[0]], averages)
+    sums, own_refs, counts = turn_call(ref_pick, best_pick, class_of[:, 0], rotated_refs, subtomograms)
+    return fused_call(own_refs, sums, counts, subtomograms, wedges)
 
 
 def solution(mesh):

time: 122 us -> 98.7 us (0.81); the launches traced: 120 us -> 98.2 us
  Pallas kernels: 107 us -> 83.7 us
  local copies, waits for them, and re-layouts: 4.51 us -> 13.9 us
  between operations: 6.14 us -> 0.68 us
  other arithmetic: 2.66 us -> 0 us
    pallas_call x3 -> x2, Pallas kernels: 107 us -> 83.7 us  [the longest x1 73.4 us: fused_call(): pl.pallas_call(fused_kernel, out_shape=(jax.ShapeDtypeStruct((STEPS, v.sh...]
    unnamed x39 -> x26, local copies, waits for them, and re-layouts: 1.98 us -> 13.9 us
    slice x2 -> x0, local copies, waits for them, and re-layouts: 1.89 us -> none  [the longest x1 1.33 us: local(): ref_pick[s] // per == orient_index]
    select_n x1 -> x0, other arithmetic: 1.43 us -> none  [local(): jnp.where(ref_pick[s] // per == orient_index, lax.dynamic_index_in_dim(ro...]
where the time goes in v2:
time: 98.7 us; the launch traced here: 98.2 us
  Pallas kernels  83.7 us (85%)
  local copies, waits for them, and re-layouts  13.9 us (14%)
    pallas_call x1, Pallas kernels, fused_call(): pl.pallas_call(fused_kernel, out_shape=(jax.ShapeDtypeStruct((STEPS, v.sh...  73.4 us
    unnamed x26, local copies, waits for them, and re-layouts  13.9 us
    pallas_call x1, Pallas kernels, turn_call(): pl.pallas_call(turn_kernel, out_shape=(jax.ShapeDtypeStruct((2, 8, 2048,...  10.3 us

profile of v2, /device:TPU:0, one launch (start us, length us, event | category | flops | bytes accessed | tf_op | source)
XLA Modules:
  0.0 98.2 jit_solution(6406109060730655412)
XLA Ops:
  0.6 0.0 copy-start
  0.6 1.9 %copy-done = bf16[6,64,4096]{2,1,0:T(8,128)(2,1)S(1)} copy-done((bf16[6,64,4096]{2,1,0:T(8,128)(2,1)S(1)}, bf16[6,64,4096]{2,1,0:T(8,128)(2,1)}, u32[]{:S(2)}) %copy-start) | copy-done | bytes 3145752
  2.5 0.0 copy-start.1
  2.5 1.6 %copy-done.1 = bf16[4,64,4096]{2,1,0:T(8,128)(2,1)S(1)} copy-done((bf16[4,64,4096]{2,1,0:T(8,128)(2,1)S(1)}, bf16[4,64,4096]{2,1,0:T(8,128)(2,1)}, u32[]{:S(2)}) %copy-start.1) | copy-done | bytes 2097176
  4.1 0.0 copy-start.3
  4.1 0.9 copy-done.3
  5.0 0.0 copy-start.4
  5.0 0.9 copy-done.4
  5.9 0.0 copy-start.5
  5.9 0.8 copy-done.5
  6.7 0.0 copy-start.6
  6.7 0.7 copy-done.6
  7.4 0.0 copy-start.7
  7.4 0.7 copy-done.7
  8.1 0.0 copy-start.9
  8.1 0.7 copy-done.9
  8.8 0.0 copy-start.10
  8.8 0.7 copy-done.10
  9.4 0.0 copy-start.11
  9.4 0.7 copy-done.11
  10.1 10.3 %shard_map.194 = (bf16[2,8,2048,128]{3,2,1,0:T(8,128)(2,1)}, bf16[2,64,4096]{2,1,0:T(8,128)(2,1)S(1)}, f32[8,128]{1,0:T(8,128)S(1)}) custom-call(s32[2]{0:T(128)S(1)} %copy-done.9, s32[6]{0:T(128)S(1)} %copy-done.10, s32[6]{0:T(128)S(1)} %bitcast.2, bf16[4,64,4096]{2,1,0:T(8,128)(2,1)S(1)} %copy-done.1, bf16[6,64,4096]{2,1,0:T(8,128)(2,1)S(1)} %copy-done, ...), custom_call_target="tpu_custom_call" | custom-call | tf_op jit(solution)/shard_map/pallas_call | solution.py:378
  20.4 0.0 copy-start.2
  20.4 1.1 %copy-done.2 = bf16[2,64,4096]{2,1,0:T(8,128)(2,1)} copy-done((bf16[2,64,4096]{2,1,0:T(8,128)(2,1)}, bf16[2,64,4096]{2,1,0:T(8,128)(2,1)S(1)}, u32[]{:S(2)}) %copy-start.2) | copy-done | bytes 1048600
  21.4 0.0 copy-start.8
  21.4 0.6 copy-done.8
  22.0 73.4 %shard_map.195 = (f32[2,6]{1,0:T(2,128)}, f32[1,8,4096]{2,1,0:T(8,128)}) custom-call(bf16[2,64,4096]{2,1,0:T(8,128)(2,1)} %copy-done.2, bf16[2,64,256,128]{3,2,1,0:T(8,128)(2,1)} %bitcast.3, f32[8,128]{1,0:T(8,128)} %copy-done.8, bf16[6,64,4096]{2,1,0:T(8,128)(2,1)} %v.3, bf16[2,64,4096]{2,1,0:T(8,128)(2,1)} %wedges.1, ...), custom_call_target="tpu_custom_call" | custom-call | tf_op jit(solution)/shard_map/pallas_call | solution.py:810
  95.4 1.2 %copy.23 = f32[2,6]{1,0:T(2,128)} copy(f32[2,6]{1,0:T(2,128)} %get-tuple-element.10) | data formatting | bytes 96
  96.6 1.6 %copy.24 = f32[1,8,4096]{2,1,0:T(8,128)} copy(f32[1,8,4096]{2,1,0:T(8,128)} %get-tuple-element.11) | data formatting | bytes 262144
Async XLA Ops:
  0.6 1.9 %copy-start = (bf16[6,64,4096]{2,1,0:T(8,128)(2,1)S(1)}, bf16[6,64,4096]{2,1,0:T(8,128)(2,1)}, u32[]{:S(2)}) copy-start(bf16[6,64,4096]{2,1,0:T(8,128)(2,1)} %v.3) | copy-start | bytes 9437188
  2.5 1.6 %copy-start.1 = (bf16[4,64,4096]{2,1,0:T(8,128)(2,1)S(1)}, bf16[4,64,4096]{2,1,0:T(8,128)(2,1)}, u32[]{:S(2)}) copy-start(bf16[4,64,4096]{2,1,0:T(8,128)(2,1)} %refs.1) | copy-start | bytes 6291460
  4.1 0.9 copy-start.3
  5.0 0.9 copy-start.4
  5.9 0.8 copy-start.5
  6.7 0.7 copy-start.6
  7.4 0.7 copy-start.7
  8.1 0.7 copy-start.9
  8.8 0.7 copy-start.10
  9.4 0.7 copy-start.11
  20.4 1.1 %copy-start.2 = (bf16[2,64,4096]{2,1,0:T(8,128)(2,1)}, bf16[2,64,4096]{2,1,0:T(8,128)(2,1)S(1)}, u32[]{:S(2)}) copy-start(bf16[2,64,4096]{2,1,0:T(8,128)(2,1)S(1)} %get-tuple-element.5.own_refs) | copy-start | bytes 3145732
  21.4 0.6 copy-start.8

commit v3 on v2

--- a/solution.py
+++ b/solution.py
@@ -52,12 +52,28 @@
     x_inv = x_fwd.T
     flip_rows = np.kron(np.diag([1.0, -1.0]), rev)
     flip_lanes = np.kron(np.eye(2), rev)
-    return [
-        np.stack([x_fwd, x_wdg]),
-        np.stack([lanes_forward(fwd), lanes_forward(wdg)]),
-        np.stack([rows_forward(fwd), rows_forward(wdg)]),
-        y_inv, z_inv, x_inv, flip_rows, flip_lanes,
-    ]
+    table = np.zeros((1408, 512))
+    for k, t in enumerate((fwd, wdg)):
+        table[512 * k:512 * k + 512] = lanes_forward(t)
+        table[1024 + 128 * k:1152 + 128 * k, 256:384] = rows_forward(t)
+    table[1024:1280, :256] = z_inv
+    table[1024:1152, 384:] = y_inv
+    table[1152:1280, 384:] = flip_rows
+    table[1280:, :128] = flip_lanes
+    table[1280:1344, 128:192] = x_fwd
+    table[1344:, 128:192] = x_wdg
+    table[1280:1344, 256:320] = x_inv
+    return table
+
+
+def table_views(table):
+    return (
+        [table.at[1280:1344, 128:192], table.at[1344:1408, 128:192]],
+        [table.at[0:512, :], table.at[512:1024, :]],
+        [table.at[1024:1152, 256:384], table.at[1152:1280, 256:384]],
+        table.at[1024:1152, 384:512], table.at[1024:1280, 0:256], table.at[1280:1344, 256:320],
+        table.at[1152:1280, 384:512], table.at[1280:1408, 0:128],
+    )
 
 
 def dot(a, b):
@@ -215,12 +231,19 @@
     lanes = np.einsum("ac,hg,zw->ahzgcw", two, two, eye).reshape(256, 256)
     rows = np.transpose(eye.reshape(N, 32, 2), (0, 2, 1)).reshape(N, N)
     flip_rows = np.stack([eye, rev])
-    flip_lanes = np.stack([np.kron(a, b) for a in (two, swap) for b in (eye, rev)])
-    return [pair, lanes, rows, flip_rows, flip_lanes]
-
-
-def turn_kernel(ref_pick, pick, classes, refs, v, pair, lanes, rows, flip_rows, flip_lanes,
+    flip_lanes = np.stack([np.kron(a, b) for b in (eye, rev) for a in (two, swap)])
+    table = np.zeros((512, 512))
+    table[:256, :256] = lanes
+    table[:, 256:384] = flip_lanes.reshape(512, 128)
+    table[:64, 384:] = pair
+    table[64:128, 384:448] = rows
+    table[128:256, 384:448] = flip_rows.reshape(128, 64)
+    return table
+
+
+def turn_kernel(ref_pick, pick, classes, refs, v, table,
                 out, own_refs, counts, held, wide, mixed, total, narrow, empty, out_sem, ref_sem):
+    pair, lanes, rows = table.at[0:64, 384:512], table.at[0:256, 0:256], table.at[64:128, 384:448]
     low = lax.broadcasted_iota(jnp.int32, (64, 128), 1) < 64
     me, per = lax.axis_index("orient"), refs.shape[0]
 
@@ -304,7 +327,8 @@
         pl.when((order == 1) | (order == 3) | (order == 5))(swap_ends)
         pl.when((order >= 1) & (order <= 4))(swap_first)
         pl.when((order == 1) | (order == 4))(swap_ends)
-        j0, jl = flip_rows[f0], flip_lanes[f1 * 2 + f2]
+        j0 = table[pl.ds(pl.multiple_of(128 + f0 * 64, 64), 64), 384:448]
+        jl = table[pl.ds(pl.multiple_of(place * 128, 128), 128), 256:384]
 
         def flip_ends(m, _):
             at = pl.ds(pl.multiple_of(m * 256, 256), 256)
@@ -373,7 +397,7 @@
 
 
 def turn_call(ref_pick, pick, classes, refs, v):
-    tables = [jnp.asarray(t, dtype=BF) for t in turn_tables()]
+    table = jnp.asarray(turn_tables(), dtype=BF)
     sm, vm, far = [pl.BlockSpec(memory_space=m) for m in (pltpu.SMEM, pltpu.VMEM, pl.ANY)]
     return pl.pallas_call(
         turn_kernel,
@@ -382,7 +406,7 @@
             jax.ShapeDtypeStruct((2,) + refs.shape[1:], BF),
             jax.ShapeDtypeStruct((8, 128), F32),
         ),
-        in_specs=[sm] * 3 + [far] + [vm] * 6,
+        in_specs=[sm] * 3 + [far] + [vm] * 2,
         out_specs=(far, vm, vm),
         scratch_shapes=[
             pltpu.VMEM((2048, 128), BF), pltpu.VMEM((2304, 128), F32), pltpu.VMEM((1024, 256), BF),
@@ -390,7 +414,7 @@
             pltpu.SemaphoreType.DMA((CLASSES,)), pltpu.SemaphoreType.DMA((2,)),
         ],
         compiler_params=pltpu.CompilerParams(vmem_limit_bytes=40 * 2**20),
-    )(ref_pick, pick, classes, refs, v, *tables)
+    )(ref_pick, pick, classes, refs, v, table)
 
 
 PARTS = (
@@ -421,12 +445,21 @@
     def partners(self):
         return [self.other_core()] + [self.device(k, t[k]) for k in range(3) for t in (self.near, self.far)]
 
+    def group(self, j):
+        return (lax.axis_index("tomo"), j * 2 + self.core)
+
+    def all_partners(self):
+        j = self.at[0] * 2 + self.at[1] % 2
+        around = [self.group((j + d) % 8) for d in range(1, 8)]
+        return around + [self.other_core(), self.device(1, self.far[1]),
+                         self.device(2, self.near[2]), self.device(2, self.far[2])]
+
 
 def greet(place):
     barrier = pltpu.get_barrier_semaphore()
-    for device in place.partners():
+    for device in place.all_partners():
         pl.semaphore_signal(barrier, inc=1, device_id=device, device_id_type=MESH)
-    pl.semaphore_wait(barrier, 7)
+    pl.semaphore_wait(barrier, 11)
 
 
 class ClassSums:
@@ -582,86 +615,61 @@
 
 
 class References:
-    def __init__(self, place, own, full, half, acc, zfirst, zsecond, pass_on, yown, ysend, ygot, send_sem, recv_sem):
-        self.p, self.own, self.full, self.half, self.acc = place, own, full, half, acc
-        self.zfirst, self.zsecond, self.pass_on = zfirst, zsecond, pass_on
-        self.yown, self.ysend, self.ygot = yown, ysend, ygot
+    ROUNDS = 4
+
+    def __init__(self, place, own, full, half, acc, got, send_sem, recv_sem):
+        self.p, self.own, self.full, self.half, self.acc, self.got = place, own, full, half, acc, got
         self.send_sem, self.recv_sem = send_sem, recv_sem
         self.sent, self.coming = [], {}
-        c = place.at[0]
-        self.c = c
-        self.f = (place.near[0], place.far[0])
-        self.g = (place.far[0], place.near[0])
-        self.h = place.cross[0]
-        self.ylo = place.at[1] % 2
+        self.j = place.at[0] * 2 + place.at[1] % 2
         self.lane = place.core * 2048
 
-    def move(self, s, k, src, dst, device):
+    def move(self, k, src, dst, device):
         copy = pltpu.make_async_remote_copy(
-            src_ref=src, dst_ref=dst, send_sem=self.send_sem.at[s * 10 + k], recv_sem=self.recv_sem.at[s * 10 + k],
+            src_ref=src, dst_ref=dst, send_sem=self.send_sem.at[k], recv_sem=self.recv_sem.at[k],
             device_id=device, device_id_type=MESH)
         copy.start()
         self.sent.append(copy)
-        self.coming[s, k] = copy
+        self.coming[k] = copy
 
     def lanes(self, at, size):
         return pl.ds(pl.multiple_of(at, 256), size)
 
-    def share(self, s, k, at, size, device):
-        cells = self.full.at[s, :, self.lanes(at, size)]
-        self.move(s, k, cells, cells, device)
+    def share(self, k, j, device):
+        cells = self.full.at[:, :, self.lanes(self.lane + j * 256, 256)]
+        self.move(k, cells, cells, device)
 
     def start(self):
         for s in range(2):
             other = self.lanes((1 - self.p.core) * 2048, 2048)
-            self.move(s, 0, self.own.at[s, :, other], self.half.at[s], self.p.other_core())
+            self.move(s, self.own.at[s, :, other], self.half.at[s], self.p.other_core())
 
     def round(self, r):
-        for s in range(2):
-            self.step(r, s)
-
-    def step(self, r, s):
-        f, g, c, h = self.f[s], self.g[s], self.c, self.h
-        to_f, to_g = self.p.device(0, f), self.p.device(0, g)
-        to_y = self.p.device(1, self.p.near[1])
-        chunk = self.lane + c * 512
         if r == 0:
-            self.coming[s, 0].wait_recv()
-            for k in range(4):
-                mine = self.own[s, :, self.lanes(self.lane + k * 512, 512)]
-                self.acc[s, k] = mine + self.half[s, :, k * 512:k * 512 + 512]
-            self.move(s, 2, self.acc.at[s, h], self.zfirst.at[s, 1], to_f)
-            self.move(s, 1, self.acc.at[s, f], self.zfirst.at[s, 0], to_f)
+            for s in range(2):
+                self.coming[s].wait_recv()
+            for k in range(8):
+                mine = self.own[:, :, self.lanes(self.lane + k * 256, 256)]
+                self.acc[k] = mine + self.half[:, :, k * 256:k * 256 + 256]
+            for d in (1, 7, 2, 6, 3, 5, 4):
+                to = (self.j + d) % 8
+                self.move(1 + d, self.acc.at[to], self.got.at[d - 1], self.p.group(to))
         elif r == 1:
-            self.coming[s, 2].wait_recv()
-            self.pass_on[s] = self.acc[s, g] + self.zfirst[s, 1]
-            self.move(s, 3, self.pass_on.at[s], self.zsecond.at[s], to_g)
+            total = self.acc[self.j]
+            for d in (1, 7, 2, 6, 3, 5, 4):
+                self.coming[1 + d].wait_recv()
+                total = total + self.got[d - 1]
+            self.full[:, :, self.lanes(self.lane + self.j * 256, 256)] = total
+            for d in (1, 7, 2, 6, 3, 5, 4):
+                self.share(8 + d, self.j, self.p.group((self.j + d) % 8))
+            self.share(16, self.j, self.p.other_core())
         elif r == 2:
-            self.coming[s, 1].wait_recv()
-            self.coming[s, 3].wait_recv()
-            v = self.acc[s, c] + self.zfirst[s, 0] + self.zsecond[s]
-            low = self.ylo == 0
-            self.yown[s] = jnp.where(low, v[:, :256], v[:, 256:])
-            self.ysend[s] = jnp.where(low, v[:, 256:], v[:, :256])
-            self.move(s, 4, self.ysend.at[s], self.ygot.at[s], to_y)
-        elif r == 3:
-            self.coming[s, 4].wait_recv()
-            at = chunk + self.ylo * 256
-            self.full[s, :, self.lanes(at, 256)] = self.yown[s] + self.ygot[s]
-            self.share(s, 5, at, 256, to_y)
-        elif r == 4:
-            self.coming[s, 5].wait_recv()
-            self.share(s, 6, chunk, 512, to_g)
-        elif r == 5:
-            self.coming[s, 6].wait_recv()
-            self.share(s, 7, chunk, 512, to_f)
-            self.share(s, 8, self.lane + g * 512, 512, to_f)
-        elif r == 6:
-            self.coming[s, 7].wait_recv()
-            self.coming[s, 8].wait_recv()
-            self.share(s, 9, self.lane, 2048, self.p.other_core())
+            for d in (1, 7, 2, 6, 3, 5, 4):
+                self.coming[8 + d].wait_recv()
+                self.share(16 + d, (self.j - d + 8) % 8, self.p.other_core())
         else:
-            self.coming[s, 9].wait_recv()
+            for d in range(8):
+                self.coming[16 + d].wait_recv()
 
     def finish(self):
         for copy in self.sent:
@@ -671,9 +679,8 @@
     def scratch():
         vm = pltpu.VMEM
         return [
-            vm((2, 64, 4096), BF), vm((2, 64, 2048), BF), vm((2, 4, 64, 512), BF), vm((2, 2, 64, 512), BF),
-            vm((2, 64, 512), BF), vm((2, 64, 512), BF), vm((2, 64, 256), BF), vm((2, 64, 256), BF), vm((2, 64, 256), BF),
-            pltpu.SemaphoreType.DMA((20,)), pltpu.SemaphoreType.DMA((20,)),
+            vm((2, 64, 4096), BF), vm((2, 64, 2048), BF), vm((8, 2, 64, 256), BF), vm((7, 2, 64, 256), BF),
+            pltpu.SemaphoreType.DMA((24,)), pltpu.SemaphoreType.DMA((24,)),
         ]
 
 
@@ -686,9 +693,9 @@
 
 
 class Scores:
-    def __init__(self, v, wedge, full, tables, out, scratch):
+    def __init__(self, v, wedge, full, table, out, scratch):
         self.v, self.wedge, self.full, self.out = v, wedge, full, out
-        self.txf, self.tzf, self.tyf, self.tyi, self.tzi, self.txi, self.fr, self.fl = tables
+        self.txf, self.tzf, self.tyf, self.tyi, self.tzi, self.txi, self.fr, self.fl = table_views(table)
         self.left, self.plane, self.spec, self.rspec, self.weight, self.edge, self.filt, self.extra = scratch
         self.low = lax.broadcasted_iota(jnp.int32, (64, 128), 1) < 64
         self.row = lax.broadcasted_iota(jnp.int32, (8, 128), 0)
@@ -701,12 +708,12 @@
 
     def forward(self, first, second, kind, out):
         def x():
-            forward_x(first, 0, self.txf[kind], self.left)
-            forward_x(second, 1, self.txf[kind], self.left)
+            forward_x(first, 0, self.txf[kind][...], self.left)
+            forward_x(second, 1, self.txf[kind][...], self.left)
         return [
             (0.6, x),
-            (0.9, lambda: forward_z(self.tzf[kind], self.left, self.plane)),
-            (0.6, lambda: forward_y(self.tyf[kind], self.plane, out)),
+            (0.9, lambda: forward_z(self.tzf[kind][...], self.left, self.plane)),
+            (0.6, lambda: forward_y(self.tyf[kind][...], self.plane, out)),
         ]
 
     def mirror(self, spec):
@@ -768,12 +775,11 @@
         action()
 
 
-REF_TIMES = (1.5, 2.4, 3.3, 4.2, 5.4, 6.3, 7.5, 9.2)
-CLASS_TIMES = ((2.2, 1.2), (10.0, 1.0), (16.0, 0.8), (21.0, 0.4), (24.0, 0.3), (26.0, 0.3), (28.0, 0.2))
-
-
-def fused_kernel(own_refs, sums, counts, v, wedges, *rest):
-    tables, (scores_out, out), scratch = rest[:8], rest[8:10], rest[10:]
+REF_TIMES = (2.0, 6.0, 9.0, 9.2)
+CLASS_TIMES = ((3.0, 0.9), (9.05, 0.02), (14.0, 0.5), (17.0, 0.4), (20, 0.3), (23, 0.3), (26, 0.2))
+
+
+def fused_kernel(own_refs, sums, counts, v, wedges, table, scores_out, out, *scratch):
     place = Place()
     ends = np.cumsum([0] + [len(c.scratch()) for c in (ClassSums, Counts, References, Scores)])
     s, tally_s, refs_s, score_s = [scratch[i:j] for i, j in zip(ends, ends[1:])]
@@ -781,7 +787,7 @@
     tally = Counts(place, counts, *tally_s)
     refs = References(place, own_refs, *refs_s)
     orient = lax.axis_index("orient")
-    scores = Scores(v, wedges.at[orient * wedges.shape[0] // lax.axis_size("orient")], refs.full, tables, scores_out, score_s)
+    scores = Scores(v, wedges.at[orient * wedges.shape[0] // lax.axis_size("orient")], refs.full, table, scores_out, score_s)
     greet(place)
     refs.start()
     tally.start()
@@ -805,17 +811,17 @@
 
 
 def fused_call(own_refs, sums, counts, v, wedges):
-    tables = [jnp.asarray(t, dtype=BF) for t in score_tables()]
+    table = jnp.asarray(score_tables(), dtype=BF)
     vm = pl.BlockSpec(memory_space=pltpu.VMEM)
     return pl.pallas_call(
         fused_kernel,
         out_shape=(jax.ShapeDtypeStruct((STEPS, v.shape[0]), F32), jax.ShapeDtypeStruct((1, 8, 4096), F32)),
-        in_specs=[vm, pl.BlockSpec(memory_space=pl.ANY)] + [vm] * 11,
+        in_specs=[vm, pl.BlockSpec(memory_space=pl.ANY)] + [vm] * 4,
         out_specs=(vm, vm),
         scratch_shapes=sum([c.scratch() for c in (ClassSums, Counts, References, Scores)], []),
         compiler_params=pltpu.CompilerParams(
             collective_id=0, has_side_effects=True, vmem_limit_bytes=60 * 2**20),
-    )(own_refs, sums.reshape(2, 64, 256, 128), counts, v, wedges, *tables)
+    )(own_refs, sums.reshape(2, 64, 256, 128), counts, v, wedges, table)
 
 
 def local(subtomograms, rotated_refs, wedges, ref_pick, best_pick, class_of):

time: 98.7 us -> 85.9 us (0.87)
  Pallas kernels: 83.7 us -> 74.1 us
  local copies, waits for them, and re-layouts: 13.9 us -> 10.9 us
    pallas_call x1, Pallas kernels: 73.4 us -> 66.6 us  [fused_call(): pl.pallas_call(fused_kernel, out_shape=(jax.ShapeDtypeStruct((STEPS, v.sh...]
    unnamed x26 -> x18, local copies, waits for them, and re-layouts: 13.9 us -> 10.9 us
    pallas_call x1, Pallas kernels: 10.3 us -> 7.44 us  [turn_call(): pl.pallas_call(turn_kernel, out_shape=(jax.ShapeDtypeStruct((2, 8, 2048,...]
where the time goes in v3:
time: 85.9 us; the launch traced here: 85.6 us
  Pallas kernels  74.1 us (86%)
  local copies, waits for them, and re-layouts  10.9 us (13%)
    pallas_call x1, Pallas kernels, fused_call(): pl.pallas_call(fused_kernel, out_shape=(jax.ShapeDtypeStruct((STEPS, v.sh...  66.6 us
    unnamed x18, local copies, waits for them, and re-layouts  10.9 us
    pallas_call x1, Pallas kernels, turn_call(): pl.pallas_call(turn_kernel, out_shape=(jax.ShapeDtypeStruct((2, 8, 2048,...  7.44 us

profile of v3, /device:TPU:0, one launch (start us, length us, event | category | flops | bytes accessed | tf_op | source)
XLA Modules:
  0.0 85.6 jit_solution(2714891185446047218)
XLA Ops:
  0.6 0.0 copy-start
  0.6 1.9 %copy-done = bf16[6,64,4096]{2,1,0:T(8,128)(2,1)S(1)} copy-done((bf16[6,64,4096]{2,1,0:T(8,128)(2,1)S(1)}, bf16[6,64,4096]{2,1,0:T(8,128)(2,1)}, u32[]{:S(2)}) %copy-start) | copy-done | bytes 3145752
  2.5 0.0 copy-start.1
  2.5 1.6 %copy-done.1 = bf16[4,64,4096]{2,1,0:T(8,128)(2,1)S(1)} copy-done((bf16[4,64,4096]{2,1,0:T(8,128)(2,1)S(1)}, bf16[4,64,4096]{2,1,0:T(8,128)(2,1)}, u32[]{:S(2)}) %copy-start.1) | copy-done | bytes 2097176
  4.1 0.0 copy-start.3
  4.1 1.0 %copy-done.3 = bf16[512,512]{1,0:T(8,128)(2,1)S(1)} copy-done((bf16[512,512]{1,0:T(8,128)(2,1)S(1)}, bf16[512,512]{1,0:T(8,128)(2,1)}, u32[]{:S(2)}) %copy-start.3) | copy-done | bytes 524312
  5.2 0.0 copy-start.5
  5.2 0.7 copy-done.5
  5.8 0.0 copy-start.6
  5.8 0.7 copy-done.6
  6.5 0.0 copy-start.7
  6.5 0.7 copy-done.7
  7.1 7.4 %shard_map.95 = (bf16[2,8,2048,128]{3,2,1,0:T(8,128)(2,1)}, bf16[2,64,4096]{2,1,0:T(8,128)(2,1)S(1)}, f32[8,128]{1,0:T(8,128)S(1)}) custom-call(s32[2]{0:T(128)S(1)} %copy-done.5, s32[6]{0:T(128)S(1)} %copy-done.6, s32[6]{0:T(128)S(1)} %bitcast.2, bf16[4,64,4096]{2,1,0:T(8,128)(2,1)S(1)} %copy-done.1, bf16[6,64,4096]{2,1,0:T(8,128)(2,1)S(1)} %copy-done, ...), custom_call_target="tpu_custom_call" | custom-call | tf_op jit(solution)/shard_map/pallas_call | solution.py:402
  14.6 0.0 copy-start.2
  14.6 1.0 %copy-done.2 = bf16[2,64,4096]{2,1,0:T(8,128)(2,1)} copy-done((bf16[2,64,4096]{2,1,0:T(8,128)(2,1)}, bf16[2,64,4096]{2,1,0:T(8,128)(2,1)S(1)}, u32[]{:S(2)}) %copy-start.2) | copy-done | bytes 1048600
  15.6 0.0 copy-start.4
  15.6 0.6 copy-done.4
  16.2 66.6 %shard_map.96 = (f32[2,6]{1,0:T(2,128)}, f32[1,8,4096]{2,1,0:T(8,128)}) custom-call(bf16[2,64,4096]{2,1,0:T(8,128)(2,1)} %copy-done.2, bf16[2,64,256,128]{3,2,1,0:T(8,128)(2,1)} %bitcast.3, f32[8,128]{1,0:T(8,128)} %copy-done.4, bf16[6,64,4096]{2,1,0:T(8,128)(2,1)} %v.3, bf16[2,64,4096]{2,1,0:T(8,128)(2,1)} %wedges.1, bf16[1408,512]{1,0:T(8,128)(2,1)} %constant.5.clone.table), custom_call_target="tpu_custom_call" | custom-call | tf_op jit(solution)/shard_map/pallas_call | solution.py:816
  82.9 1.2 %copy.12 = f32[2,6]{1,0:T(2,128)} copy(f32[2,6]{1,0:T(2,128)} %get-tuple-element.10) | data formatting | bytes 96
  84.1 1.6 %copy.13 = f32[1,8,4096]{2,1,0:T(8,128)} copy(f32[1,8,4096]{2,1,0:T(8,128)} %get-tuple-element.11) | data formatting | bytes 262144
Async XLA Ops:
  0.6 1.9 %copy-start = (bf16[6,64,4096]{2,1,0:T(8,128)(2,1)S(1)}, bf16[6,64,4096]{2,1,0:T(8,128)(2,1)}, u32[]{:S(2)}) copy-start(bf16[6,64,4096]{2,1,0:T(8,128)(2,1)} %v.3) | copy-start | bytes 9437188
  2.5 1.6 %copy-start.1 = (bf16[4,64,4096]{2,1,0:T(8,128)(2,1)S(1)}, bf16[4,64,4096]{2,1,0:T(8,128)(2,1)}, u32[]{:S(2)}) copy-start(bf16[4,64,4096]{2,1,0:T(8,128)(2,1)} %refs.1) | copy-start | bytes 6291460
  4.1 1.0 %copy-start.3 = (bf16[512,512]{1,0:T(8,128)(2,1)S(1)}, bf16[512,512]{1,0:T(8,128)(2,1)}, u32[]{:S(2)}) copy-start(bf16[512,512]{1,0:T(8,128)(2,1)} %constant.4.clone.table) | copy-start | bytes 1572868
  5.2 0.7 copy-start.5
  5.8 0.7 copy-start.6
  6.5 0.7 copy-start.7
  14.6 1.1 %copy-start.2 = (bf16[2,64,4096]{2,1,0:T(8,128)(2,1)}, bf16[2,64,4096]{2,1,0:T(8,128)(2,1)S(1)}, u32[]{:S(2)}) copy-start(bf16[2,64,4096]{2,1,0:T(8,128)(2,1)S(1)} %get-tuple-element.5.own_refs) | copy-start | bytes 3145732
  15.6 0.6 copy-start.4

commit v4 on v3

--- a/solution.py
+++ b/solution.py
@@ -413,7 +413,7 @@
             pltpu.VMEM((2560, 128), F32), pltpu.VMEM((6, 2048, 128), BF), pltpu.VMEM((2048, 128), BF),
             pltpu.SemaphoreType.DMA((CLASSES,)), pltpu.SemaphoreType.DMA((2,)),
         ],
-        compiler_params=pltpu.CompilerParams(vmem_limit_bytes=40 * 2**20),
+        compiler_params=pltpu.CompilerParams(vmem_limit_bytes=60 * 2**20),
     )(ref_pick, pick, classes, refs, v, table)
 
 
@@ -752,7 +752,7 @@
         ]
 
     def finish(self):
-        self.out[...] = self.result[:self.out.shape[0], :self.out.shape[1]]
+        self.out[...] = self.result
 
     @staticmethod
     def scratch():
@@ -764,19 +764,26 @@
 
 
 def interleave(work, events):
-    events = sorted(events, key=lambda e: e[0])
-    clock = 0.0
-    for length, piece in work:
-        while events and events[0][0] <= clock:
-            events.pop(0)[1]()
+    done = 0
+    for before, action in events:
+        while done < before:
+            work[done][1]()
+            done += 1
+        action()
+    for _, piece in work[done:]:
         piece()
-        clock += length
-    for _, action in events:
-        action()
-
-
-REF_TIMES = (2.0, 6.0, 9.0, 9.2)
-CLASS_TIMES = ((3.0, 0.9), (9.05, 0.02), (14.0, 0.5), (17.0, 0.4), (20, 0.3), (23, 0.3), (26, 0.2))
+
+
+ORDER = (
+    (3, -1, 0), (6, 0, 0), (7, 1, 0), (9, 2, 0), (10, 3, 0), (10, -1, 1),
+    (11, 4, 0), (13, 5, 0), (15, 0, 1), (15, 1, 1), (15, 2, 1), (15, 3, 1),
+    (15, 4, 1), (15, 5, 1), (15, -1, 2), (15, -1, 3), (20, 0, 2), (21, 1, 2),
+    (21, 2, 2), (22, 3, 2), (23, 4, 2), (23, 5, 2), (24, 0, 3), (25, 1, 3),
+    (25, 2, 3), (26, 3, 3), (26, 4, 3), (27, 5, 3), (29, 0, 4), (29, 1, 4),
+    (30, 2, 4), (30, 3, 4), (30, 4, 4), (30, 5, 4), (33, 0, 5), (33, 1, 5),
+    (33, 2, 5), (33, 3, 5), (34, 4, 5), (34, 5, 5), (36, 0, 6), (36, 1, 6),
+    (37, 2, 6), (37, 3, 6), (37, 4, 6), (38, 5, 6),
+)
 
 
 def fused_kernel(own_refs, sums, counts, v, wedges, table, scores_out, out, *scratch):
@@ -792,10 +799,11 @@
     refs.start()
     tally.start()
     classes.start()
-    events = [(t, functools.partial(refs.round, r)) for r, t in enumerate(REF_TIMES)]
-    for r, (t, gap) in enumerate(CLASS_TIMES):
-        events += [(t + gap * part, functools.partial(classes.step, r, part)) for part in range(len(PARTS))]
-        events.append((t + gap * len(PARTS), functools.partial(tally.round, r)))
+    events = []
+    for before, part, r in ORDER:
+        events.append((before, functools.partial(refs.round, r) if part < 0 else functools.partial(classes.step, r, part)))
+        if part == len(PARTS) - 1:
+            events.append((before, functools.partial(tally.round, r)))
     work = scores.wedge_work()
     for pair in range(3):
         work += scores.pair_work(pair)
@@ -815,7 +823,7 @@
     vm = pl.BlockSpec(memory_space=pltpu.VMEM)
     return pl.pallas_call(
         fused_kernel,
-        out_shape=(jax.ShapeDtypeStruct((STEPS, v.shape[0]), F32), jax.ShapeDtypeStruct((1, 8, 4096), F32)),
+        out_shape=(jax.ShapeDtypeStruct((8, 128), F32), jax.ShapeDtypeStruct((1, 8, 4096), F32)),
         in_specs=[vm, pl.BlockSpec(memory_space=pl.ANY)] + [vm] * 4,
         out_specs=(vm, vm),
         scratch_shapes=sum([c.scratch() for c in (ClassSums, Counts, References, Scores)], []),
@@ -826,7 +834,8 @@
 
 def local(subtomograms, rotated_refs, wedges, ref_pick, best_pick, class_of):
     sums, own_refs, counts = turn_call(ref_pick, best_pick, class_of[:, 0], rotated_refs, subtomograms)
-    return fused_call(own_refs, sums, counts, subtomograms, wedges)
+    scores, averages = fused_call(own_refs, sums, counts, subtomograms, wedges)
+    return (scores[:STEPS, :subtomograms.shape[0]], averages)
 
 
 def solution(mesh):

time: 85.9 us -> 78.2 us (0.910)
  local copies, waits for them, and re-layouts: 10.9 us -> 2.8 us
    unnamed x18 -> x1, local copies, waits for them, and re-layouts: 10.9 us -> 1.57 us
    pallas_call x1, Pallas kernels: 7.44 us -> 12.4 us  [turn_call(): pl.pallas_call(turn_kernel, out_shape=(jax.ShapeDtypeStruct((2, 8, 2048,...]
    pallas_call x1, Pallas kernels: 66.6 us -> 61.9 us  [fused_call(): pl.pallas_call(fused_kernel, out_shape=(jax.ShapeDtypeStruct((8, 128), F3...]
    slice x0 -> x1, local copies, waits for them, and re-layouts: none -> 1.24 us  [local(): return (scores[:STEPS, :subtomograms.shape[0]], averages)]
where the time goes in v4:
time: 78.2 us; the launch traced here: 77.8 us
  Pallas kernels  74.4 us (95%)
  local copies, waits for them, and re-layouts  2.8 us (4%)
    pallas_call x1, Pallas kernels, fused_call(): pl.pallas_call(fused_kernel, out_shape=(jax.ShapeDtypeStruct((8, 128), F3...  61.9 us
    pallas_call x1, Pallas kernels, turn_call(): pl.pallas_call(turn_kernel, out_shape=(jax.ShapeDtypeStruct((2, 8, 2048,...  12.4 us
    unnamed x1, local copies, waits for them, and re-layouts  1.57 us

profile of v4, /device:TPU:0, one launch (start us, length us, event | category | flops | bytes accessed | tf_op | source)
XLA Modules:
  0.0 77.8 jit_solution(16652203190096168680)
XLA Ops:
  0.6 12.4 %shard_map.95 = (bf16[2,8,2048,128]{3,2,1,0:T(8,128)(2,1)}, bf16[2,64,4096]{2,1,0:T(8,128)(2,1)}, f32[8,128]{1,0:T(8,128)}) custom-call(s32[2]{0:T(128)} %ref_pick.1, s32[6]{0:T(128)} %pick.1, s32[6]{0:T(128)} %bitcast.3, bf16[4,64,4096]{2,1,0:T(8,128)(2,1)} %refs.1, bf16[6,64,4096]{2,1,0:T(8,128)(2,1)} %v.3, bf16[512,512]{1,0:T(8,128)(2,1)} %constant.4.clone.table), custom_call_target="tpu_custom_call" | custom-call | tf_op jit(solution)/shard_map/pallas_call | solution.py:402
  13.1 61.9 %shard_map.96 = (f32[8,128]{1,0:T(8,128)}, f32[1,8,4096]{2,1,0:T(8,128)}) custom-call(bf16[2,64,4096]{2,1,0:T(8,128)(2,1)} %get-tuple-element.7.own_refs, bf16[2,64,256,128]{3,2,1,0:T(8,128)(2,1)} %bitcast.2, f32[8,128]{1,0:T(8,128)} %get-tuple-element.9.counts, bf16[6,64,4096]{2,1,0:T(8,128)(2,1)} %v.3, bf16[2,64,4096]{2,1,0:T(8,128)(2,1)} %wedges.1, ...), custom_call_target="tpu_custom_call" | custom-call | tf_op jit(solution)/shard_map/pallas_call | solution.py:824
  75.0 1.2 %slice.3 = f32[2,6]{1,0:T(2,128)} slice(f32[8,128]{1,0:T(8,128)} %get-tuple-element.10), slice={[0:2], [0:6]} | slice | bytes 96 | tf_op jit(solution)/shard_map/slice | solution.py:838
  76.2 1.6 %copy.11 = f32[1,8,4096]{2,1,0:T(8,128)} copy(f32[1,8,4096]{2,1,0:T(8,128)} %get-tuple-element.15) | data formatting | bytes 262144

commit v5 on v4

--- a/solution.py
+++ b/solution.py
@@ -760,6 +760,7 @@
         return [
             vm((2048, 512), BF), vm((4608, 128), F32), vm((3, 4096, 128), BF), vm((4096, 128), BF),
             vm((2048, 128), F32), vm((128, 128), F32), vm((2, 4096, 128), F32), vm((2, 128, 128), F32),
+            vm((64, 4096), BF), vm((6, 64, 4096), BF), pltpu.SemaphoreType.DMA((2,)),
         ]
 
 
@@ -794,11 +795,19 @@
     tally = Counts(place, counts, *tally_s)
     refs = References(place, own_refs, *refs_s)
     orient = lax.axis_index("orient")
-    scores = Scores(v, wedges.at[orient * wedges.shape[0] // lax.axis_size("orient")], refs.full, table, scores_out, score_s)
+    wedge_in, v_in, in_sem = score_s[-3:]
+    wedge_copy = pltpu.make_async_copy(
+        wedges.at[orient * wedges.shape[0] // lax.axis_size("orient")], wedge_in, in_sem.at[0])
+    v_copy = pltpu.make_async_copy(v, v_in, in_sem.at[1])
+    scores = Scores(v_in, wedge_in, refs.full, table, scores_out, score_s[:-3])
+    wedge_copy.start()
+    v_copy.start()
     greet(place)
     refs.start()
     tally.start()
     classes.start()
+    wedge_copy.wait()
+    v_copy.wait()
     events = []
     for before, part, r in ORDER:
         events.append((before, functools.partial(refs.round, r) if part < 0 else functools.partial(classes.step, r, part)))
@@ -820,11 +829,11 @@
 
 def fused_call(own_refs, sums, counts, v, wedges):
     table = jnp.asarray(score_tables(), dtype=BF)
-    vm = pl.BlockSpec(memory_space=pltpu.VMEM)
+    vm, far = pl.BlockSpec(memory_space=pltpu.VMEM), pl.BlockSpec(memory_space=pl.ANY)
     return pl.pallas_call(
         fused_kernel,
         out_shape=(jax.ShapeDtypeStruct((8, 128), F32), jax.ShapeDtypeStruct((1, 8, 4096), F32)),
-        in_specs=[vm, pl.BlockSpec(memory_space=pl.ANY)] + [vm] * 4,
+        in_specs=[vm, far, vm, far, far, vm],
         out_specs=(vm, vm),
         scratch_shapes=sum([c.scratch() for c in (ClassSums, Counts, References, Scores)], []),
         compiler_params=pltpu.CompilerParams(

time: 78.2 us -> 77.1 us (0.986)
    pallas_call x1, Pallas kernels: 61.9 us -> 60.6 us  [fused_call(): pl.pallas_call(fused_kernel, out_shape=(jax.ShapeDtypeStruct((8, 128), F3...]
where the time goes in v5:
time: 77.1 us
  Pallas kernels  73.7 us (96%)
  local copies, waits for them, and re-layouts  2.8 us (4%)
    pallas_call x1, Pallas kernels, fused_call(): pl.pallas_call(fused_kernel, out_shape=(jax.ShapeDtypeStruct((8, 128), F3...  60.6 us
    pallas_call x1, Pallas kernels, turn_call(): pl.pallas_call(turn_kernel, out_shape=(jax.ShapeDtypeStruct((2, 8, 2048,...  13.1 us
    unnamed x1, local copies, waits for them, and re-layouts  1.57 us

profile of v5, /device:TPU:0, one launch (start us, length us, event | category | flops | bytes accessed | tf_op | source)
XLA Modules:
  0.0 77.1 jit_solution(2013898692962723700)
XLA Ops:
  0.6 13.1 %shard_map.95 = (bf16[2,8,2048,128]{3,2,1,0:T(8,128)(2,1)}, bf16[2,64,4096]{2,1,0:T(8,128)(2,1)}, f32[8,128]{1,0:T(8,128)}) custom-call(s32[2]{0:T(128)} %ref_pick.1, s32[6]{0:T(128)} %pick.1, s32[6]{0:T(128)} %bitcast.3, bf16[4,64,4096]{2,1,0:T(8,128)(2,1)} %refs.1, bf16[6,64,4096]{2,1,0:T(8,128)(2,1)} %v.3, bf16[512,512]{1,0:T(8,128)(2,1)} %constant.4.clone.table), custom_call_target="tpu_custom_call" | custom-call | tf_op jit(solution)/shard_map/pallas_call | solution.py:402
  13.7 60.6 %shard_map.96 = (f32[8,128]{1,0:T(8,128)}, f32[1,8,4096]{2,1,0:T(8,128)}) custom-call(bf16[2,64,4096]{2,1,0:T(8,128)(2,1)} %get-tuple-element.7.own_refs, bf16[2,64,256,128]{3,2,1,0:T(8,128)(2,1)} %bitcast.2, f32[8,128]{1,0:T(8,128)} %get-tuple-element.9.counts, bf16[6,64,4096]{2,1,0:T(8,128)(2,1)} %v.3, bf16[2,64,4096]{2,1,0:T(8,128)(2,1)} %wedges.1, ...), custom_call_target="tpu_custom_call" | custom-call | tf_op jit(solution)/shard_map/pallas_call | solution.py:833
  74.3 1.2 %slice.3 = f32[2,6]{1,0:T(2,128)} slice(f32[8,128]{1,0:T(8,128)} %get-tuple-element.10), slice={[0:2], [0:6]} | slice | bytes 96 | tf_op jit(solution)/shard_map/slice | solution.py:847
  75.6 1.6 %copy.11 = f32[1,8,4096]{2,1,0:T(8,128)} copy(f32[1,8,4096]{2,1,0:T(8,128)} %get-tuple-element.15) | data formatting | bytes 262144
